TPU v7x, 512 devices: a whole 4x8x8 slice. The times are simulated.
512 devices in a mesh: dp: 8 (over z), seq: 8 (over x, core), enc: 8 (over y).
Axes of the slice: x: 4, y: 8, z: 8, core: 2. Of those that a mesh axis runs over, the one named last changes fastest.
Arguments:
- queries: bfloat16 [32768, 2048], P(('dp', 'seq'), 'enc'), may hold values from -6 to 6
- out_grad: bfloat16 [32768, 2048], P(('dp', 'seq'), 'enc'), may hold values from -96 to 96
- keys: bfloat16 [1024, 128, 2048], P(('dp', 'seq'), None, 'enc'), may hold values from -6 to 6
- values: bfloat16 [1024, 128, 2048], P(('dp', 'seq'), None, 'enc'), may hold values from -6 to 6
- neighbour_ids: int32 [512, 2], P(('dp', 'seq')), may hold values from 0 to 15
- neighbour_place: int32 [64, 16], P(('dp', 'seq')), may hold values from 0 to 15, each once within a row
- kv_weight: bfloat16 [2, 896, 2048], P(None, ('dp', 'seq'), 'enc'), may hold values from -0.125 to 0.125
Outputs:
- queries_grad: bfloat16 [32768, 2048], P(('dp', 'seq'), 'enc')
- encoded_grad: bfloat16 [1024, 128, 896], P(('dp', 'seq', 'enc'))
Inputs may be any that keep to these rules, and one draw needn't show every extreme that they name: `neighbour_ids`: numbers of neighbours in the span's own batch group; several slots may name the same one. `neighbour_place`: each row is a permutation; store position p lies on owner p // 2 of the group, at entry p % 2.
All inputs are finite; a program needn't handle non-finite values.
Results may differ from a plain program's by a relative error of at most 0.014.
Values may be sent and summed in bfloat16 or wider, within the bound.
No kernel may reach another device: no remote copies, remote signals or barrier semaphores. Data moves between devices by JAX's collectives and lax.ppermute only.
A program may use at most 64 MiB of HBM per device.

v0:
```python
import math

import jax
import jax.numpy as jnp
from jax import lax
from jax.sharding import PartitionSpec as P

HD = 128
SPAN = 64
NBT = 128
NEIGH = 2


def attention_back(queries, out_grad, keys, values, heads_dev):
    span_count = queries.shape[0] // SPAN
    factor = 1.0 / math.sqrt(HD)
    query_blocks = queries.reshape(span_count, SPAN, heads_dev, HD)
    grad_blocks = out_grad.reshape(span_count, SPAN, heads_dev, HD)
    key_blocks = keys.reshape(span_count, NEIGH * NBT, heads_dev, HD)
    value_blocks = values.reshape(span_count, NEIGH * NBT, heads_dev, HD)
    scores = (
        jnp.einsum("cqhd,ckhd->chqk", query_blocks, key_blocks, preferred_element_type=jnp.float32)
        * factor
    )
    row_max = jnp.max(scores, axis=-1, keepdims=True)
    exponent = jnp.exp(scores - row_max)
    weights = exponent / jnp.sum(exponent, axis=-1, keepdims=True)
    weights_low = weights.astype(jnp.bfloat16)
    attended = jnp.einsum(
        "chqk,ckhd->cqhd", weights_low, value_blocks, preferred_element_type=jnp.float32
    )
    delta = jnp.sum(attended * grad_blocks.astype(jnp.float32), axis=-1)
    delta = jnp.transpose(delta, (0, 2, 1))[..., None]
    weight_grad = jnp.einsum(
        "cqhd,ckhd->chqk", grad_blocks, value_blocks, preferred_element_type=jnp.float32
    )
    score_low = (weights * (weight_grad - delta)).astype(jnp.bfloat16)
    query_grad = (
        jnp.einsum("chqk,ckhd->cqhd", score_low, key_blocks, preferred_element_type=jnp.float32)
        * factor
    )
    key_grad = (
        jnp.einsum("chqk,cqhd->ckhd", score_low, query_blocks, preferred_element_type=jnp.float32)
        * factor
    )
    value_grad = jnp.einsum(
        "chqk,cqhd->ckhd", weights_low, grad_blocks, preferred_element_type=jnp.float32
    )
    width_dev = heads_dev * HD
    query_grad = query_grad.reshape(span_count * SPAN, width_dev).astype(jnp.bfloat16)
    key_grad = key_grad.reshape(span_count * NEIGH, NBT, width_dev)
    value_grad = value_grad.reshape(span_count * NEIGH, NBT, width_dev)
    return (query_grad, key_grad, value_grad)


def neighbour_sums(key_grad, value_grad, group_ids, place_row):
    store_size = place_row.shape[0]
    entry_index = jnp.arange(store_size, dtype=jnp.int32)
    flat_ids = group_ids.reshape(-1)
    slot_place = jnp.sum(
        jnp.where(flat_ids[:, None] == entry_index[None, :], place_row[None, :], 0), axis=1
    )
    selector = (entry_index[:, None] == slot_place[None, :]).astype(jnp.float32)
    stacked = jnp.stack([key_grad, value_grad])
    sums = jnp.einsum("ps,kstf->kptf", selector, stacked, precision=lax.Precision.HIGHEST)
    return sums.astype(jnp.bfloat16)


def local(queries, out_grad, keys, values, neighbour_ids, neighbour_place, kv_weight):
    heads_dev = queries.shape[1] // HD
    width_dev = heads_dev * HD
    query_grad, key_grad, value_grad = attention_back(queries, out_grad, keys, values, heads_dev)
    store = neighbour_sums(key_grad, value_grad, neighbour_ids, neighbour_place[0])
    enc_count = lax.axis_size("enc")
    routed = lax.all_to_all(store, "enc", split_axis=1, concat_axis=3, tiled=True)
    owned = routed.shape[1]
    columns = lax.all_gather(kv_weight, "enc", axis=2, tiled=True)
    piece = lax.all_gather(columns, ("dp", "seq"), axis=1, tiled=True)
    row_count = piece.shape[1]
    spread = routed.reshape(2, owned, NBT, enc_count, width_dev)
    weight_rows = piece.reshape(2, row_count, enc_count, width_dev)
    partial_value = jnp.einsum(
        "kpthf,kdhf->hptd", spread, weight_rows, preferred_element_type=jnp.float32
    )
    partial_value = lax.optimization_barrier(partial_value.astype(jnp.bfloat16)).astype(jnp.float32)
    encoded = jnp.sum(partial_value, axis=0)
    return (query_grad, encoded.astype(jnp.bfloat16))


def solution(mesh):
    placed = (
        P(("dp", "seq"), "enc"),
        P(("dp", "seq"), "enc"),
        P(("dp", "seq"), None, "enc"),
        P(("dp", "seq"), None, "enc"),
        P(("dp", "seq"), None),
        P(("dp", "seq"), None),
        P(None, ("dp", "seq"), "enc"),
    )
    return jax.shard_map(
        local,
        mesh=mesh,
        in_specs=placed,
        out_specs=(P(("dp", "seq"), "enc"), P(("dp", "seq", "enc"), None, None)),
        check_vma=False,
    )
```

profile of v0, /device:TPU:1, one launch (start us, length us, event | category | flops | bytes accessed | tf_op | source)
XLA Modules:
  0.0 153.8 jit_solution(7347899099590010574)
XLA Ops:
  7.2 0.0 all-gather.2.cloned.1.call-start
  7.2 15.9 %all_gather.6 = bf16[2,14,2048]{2,0,1:T(2,128)(2,1)} all-gather(bf16[2,14,256]{2,0,1:T(2,128)(2,1)} %param.13), channel_id=1, replica_groups=mesh['dp'=8,'seq'=8,'enc'=8] {'enc'}, dimensions={2}, use_global_device_ids=true | all-gather | bytes 129024 | tf_op jit(solution)/shard_map/all_gather | solution.py:77
  23.1 0.8 copy.67
  23.9 0.1 eq.29
  23.9 1.0 reshape.30
  25.0 1.1 reshape.28
  26.1 1.3 reshape.29
  27.4 1.1 reshape.31
  28.6 0.5 convolution_multiply_fusion
  29.1 1.3 fusion.34
  30.4 3.6 %convolution_bitcast_fusion = f32[8,256,2,128]{3,1,2,0:T(8,128)} fusion(bf16[8,64,2,128]{3,2,1,0:T(2,128)(2,1)S(1)} %reshape.30, f32[8,2,64]{2,1,0:T(2,128)S(1)} %get-tuple-element.2, f32[8,2,64,256]{3,2,1,0:T(8,128)S(1)} %convolution_multiply_fusion), kind=kOutput, calls=%fused_computation.10 | convolution fusion | flops 67896576 | bytes 3411968 | tf_op jit(solution)/shard_map/chqk,cqhd->ckhd/dot_general | solution.py:46
  34.0 2.2 %copy.64 = f32[8,256,2,128]{1,0,3,2:T(8,128)S(1)} copy(f32[8,256,2,128]{3,1,2,0:T(8,128)} %convolution_bitcast_fusion) | data formatting | bytes 4194304 | tf_op jit(solution)/shard_map/chqk,cqhd->ckhd/transpose | solution.py:46
  36.2 1.5 stack_reshape.7
  37.7 2.3 %copy.66 = f32[1,16,128,256]{3,1,2,0:T(8,128)S(1)} copy(f32[1,16,128,256]{2,1,3,0:T(8,128)} %stack_reshape.7) | data formatting | bytes 4194304 | tf_op jit(solution)/shard_map/stack;reshape | solution.py:64
  40.0 3.9 %fusion.17 = f32[8,64,2]{1,2,0:T(2,128)S(1)} fusion(bf16[8,256,2,128]{3,2,1,0:T(2,128)(2,1)} %reshape.31, bf16[8,64,2,128]{3,2,1,0:T(2,128)(2,1)} %copy-done.3, f32[8,2,64]{2,1,0:T(2,128)S(1)} %get-tuple-element.2, f32[8,2,64,256]{3,2,1,0:T(8,128)} %copy-done), kind=kOutput, calls=%fused_computation.21 | convolution fusion | flops 68288768 | bytes 2367488 | tf_op jit(solution)/shard_map/chqk,ckhd->cqhd/dot_general | solution.py:29
  43.9 2.2 %fusion.14 = bf16[8,2,64,256]{3,2,1,0:T(8,128)(2,1)S(1)} fusion(bf16[8,256,2,128]{3,2,1,0:T(2,128)(2,1)} %reshape.31, f32[8,2,64]{2,1,0:T(2,128)S(1)} %bitcast.54, f32[8,2,64,256]{3,2,1,0:T(8,128)} %get-tuple-element.3, f32[8,2,64]{2,1,0:T(2,128)S(1)} %get-tuple-element.2, bf16[8,64,2,128]{3,2,1,0:T(2,128)(2,1)} %copy-done.3), kind=kOutput, calls=%fused_computation.16 | convolution fusion | flops 68157440 | bytes 2891776 | tf_op jit(solution)/shard_map/cqhd,ckhd->chqk/dot_general | solution.py:34
  46.1 0.8 copy-done.2
  46.9 1.8 %multiply_bitcast_fusion = f32[8,256,2,128]{3,1,2,0:T(8,128)} fusion(bf16[8,2,64,256]{3,2,1,0:T(8,128)(2,1)S(1)} %fusion.14, bf16[8,64,2,128]{3,2,1,0:T(2,128)(2,1)S(1)} %reshape.28), kind=kOutput, calls=%fused_computation.9 | convolution fusion | flops 67633152 | bytes 2883584 | tf_op jit(solution)/shard_map/chqk,cqhd->ckhd/dot_general | solution.py:43
  48.7 3.1 %copy.62 = f32[8,256,2,128]{1,0,3,2:T(8,128)} copy(f32[8,256,2,128]{3,1,2,0:T(8,128)} %multiply_bitcast_fusion) | data formatting | bytes 4194304 | tf_op jit(solution)/shard_map/mul | solution.py:43
  51.8 2.6 %stack_reshape.6 = f32[1,16,128,256]{2,1,3,0:T(8,128)} reshape(f32[8,256,2,128]{1,0,3,2:T(8,128)} %copy.62) | data formatting | bytes 4194304 | tf_op jit(solution)/shard_map/stack;reshape | solution.py:64
  54.4 3.2 %copy.65 = f32[1,16,128,256]{3,1,2,0:T(8,128)} copy(f32[1,16,128,256]{2,1,3,0:T(8,128)} %stack_reshape.6) | data formatting | bytes 4194304 | tf_op jit(solution)/shard_map/stack;reshape | solution.py:64
  57.6 0.2 select_reduce_fusion
  57.8 3.8 %convert_bitcast_fusion = bf16[2,16,128,256]{3,1,2,0:T(8,128)(2,1)S(1)} fusion(f32[1,16,128,256]{3,1,2,0:T(8,128)S(1)} %copy.66, f32[1,16,128,256]{3,1,2,0:T(8,128)} %copy.65, s32[16]{0:T(128)S(1)} %select_reduce_fusion), kind=kOutput, calls=%fused_computation.8 | convolution fusion | flops 203424000 | bytes 6291520 | tf_op jit(solution)/shard_map/ps,kstf->kptf/dot_general | solution.py:65
  61.6 2.1 %copy.68 = bf16[2,16,128,256]{3,2,0,1:T(8,128)(2,1)} copy(bf16[2,16,128,256]{3,1,2,0:T(8,128)(2,1)S(1)} %convert_bitcast_fusion) | data formatting | bytes 4194304 | tf_op jit(solution)/shard_map/convert_element_type | solution.py:66
  63.7 4.0 %all-to-all-start = ((bf16[2,16,128,256]{3,2,0,1:T(8,128)(2,1)}), bf16[2,16,128,256]{3,2,0,1:T(8,128)(2,1)S(1)}, u32[]{:S(2)}, u32[]{:S(2)}) async-start(bf16[2,16,128,256]{3,2,0,1:T(8,128)(2,1)} %copy.68), calls=%async_computation | async-start | bytes 4194304 | tf_op jit(solution)/shard_map/all_to_all | solution.py:75
  67.7 1.3 fusion.18
  69.0 0.3 copy.60
  69.3 0.7 copy.99
  70.0 47.5 %all-gather.2.cloned.1.call-done = bf16[2,896,2048]{2,0,1:T(2,128)(2,1)} async-done(((bf16[2,14,2048]{2,0,1:T(2,128)(2,1)}), bf16[2,896,2048]{2,0,1:T(2,128)(2,1)}) %all-gather.2.cloned.1.call-update) | async-done | bytes 7340048 | tf_op jit(solution)/shard_map/all_gather | solution.py:78
  117.5 18.8 %copy.69 = bf16[2,896,2048]{1,2,0:T(8,128)(2,1)} copy(bf16[2,896,2048]{2,0,1:T(2,128)(2,1)} %all-gather.2.cloned.1.call-done) | data formatting | bytes 14680064 | tf_op jit(solution)/shard_map/all_gather | solution.py:78
  136.3 7.2 %bitcast_convert_fusion = bf16[8,2,128,896]{3,2,1,0:T(8,128)(2,1)} fusion(bf16[2,2,128,8,256]{4,2,0,1,3:T(8,128)(2,1)S(1)} %bitcast.50, bf16[2,896,8,256,1]{1,3,2,0,4:T(8,128)(2,1)} %bitcast.49), kind=kOutput, calls=%fused_computation.1 | convolution fusion | flops 1880883200 | bytes 13107200 | tf_op jit(solution)/shard_map/kpthf,kdhf->hptd/dot_general | solution.py:82
  143.5 3.4 %reduce_sum.42 = bf16[2,128,896]{2,1,0:T(8,128)(2,1)} reduce(bf16[8,2,128,896]{3,2,1,0:T(8,128)(2,1)} %bitcast_convert_fusion, bf16[]{:T(256)} %constant.4.clone.1), dimensions={0}, to_apply=%region_4.5 | reduce | flops 1605632 | bytes 4128770 | tf_op jit(solution)/shard_map/reduce_sum | solution.py:86
  (11 shorter events, 0.0 us)
Async XLA Ops:
  7.2 20.3 %copy-start.1 = (bf16[16,128,256]{2,1,0:T(8,128)(2,1)S(1)}, bf16[16,128,256]{2,1,0:T(8,128)(2,1)}, u32[]{:S(2)}) copy-start(bf16[16,128,256]{2,1,0:T(8,128)(2,1)} %param.10) | copy-start | bytes 3145732
  7.2 110.3 %all-gather.2.cloned.1.call-start = ((), (), s32[]{:S(2)}) async-start(), calls=%async_computation.1 | async-start | bytes 7454720 | tf_op jit(solution)/shard_map/all_gather | solution.py:78
  25.0 5.4 %copy-start.3 = (bf16[8,64,2,128]{3,2,1,0:T(2,128)(2,1)}, bf16[8,64,2,128]{3,2,1,0:T(2,128)(2,1)S(1)}, u32[]{:S(2)}) copy-start(bf16[8,64,2,128]{3,2,1,0:T(2,128)(2,1)S(1)} %reshape.30) | copy-start | bytes 786436
  29.1 1.3 copy-start
  46.1 0.8 copy-start.2
  54.4 3.2 %copy-start.4 = (s32[1,16]{1,0:T(1,128)S(1)}, s32[1,16]{1,0:T(1,128)}, u32[]{:S(2)}) copy-start(s32[1,16]{1,0:T(1,128)} %param.12) | copy-start | bytes 196
  63.7 72.6 %all-to-all-start = ((bf16[2,16,128,256]{3,2,0,1:T(8,128)(2,1)}), bf16[2,16,128,256]{3,2,0,1:T(8,128)(2,1)S(1)}, u32[]{:S(2)}, u32[]{:S(2)}) async-start(bf16[2,16,128,256]{3,2,0,1:T(8,128)(2,1)} %copy.68), calls=%async_computation | async-start | bytes 4194304 | tf_op jit(solution)/shard_map/all_to_all | solution.py:75
Sparse Core Ops, SparseCore 0:
  23.2 94.2 all-gather.1
where the time goes:
time: 155 us; the launch traced here: 154 us
  waiting for transfers between devices  47.5 us (31%)
  local copies, waits for them, and re-layouts  43.1 us (28%)
  matrix products  24.3 us (16%)
  blocking collectives  15.9 us (10%)
  between operations  14.1 us (9%)
  other arithmetic  4.9 us (3%)
  starting transfers between devices  4.02 us (3%)
    all_gather x1, waiting for transfers between devices, local(): piece = lax.all_gather(columns, ('dp', 'seq'), axis=1, tiled=True)  47.5 us
    all_gather x1, local copies, waits for them, and re-layouts, local(): piece = lax.all_gather(columns, ('dp', 'seq'), axis=1, tiled=True)  18.8 us
    all_gather x1, blocking collectives, local(): columns = lax.all_gather(kv_weight, 'enc', axis=2, tiled=True)  15.9 us
    another operation x4, local copies, waits for them, and re-layouts, neighbour_sums(): stacked = jnp.stack([key_grad, value_grad])  9.63 us
    dot_general x1, matrix products, local(): jnp.einsum('kpthf,kdhf->hptd', spread, weight_rows, preferred_element_typ...  7.23 us
    all_to_all x1, starting transfers between devices, local(): lax.all_to_all(store, 'enc', split_axis=1, concat_axis=3, tiled=True)  3.98 us
    dot_general x1, matrix products, attention_back(): jnp.einsum('chqk,ckhd->cqhd', weights_low, value_blocks, preferred_elemen...  3.89 us
    dot_general x1, matrix products, neighbour_sums(): jnp.einsum('ps,kstf->kptf', selector, stacked, precision=lax.Precision.HI...  3.78 us
  transfers between devices with their start and end apart: 2, of which 1 were waited for; matrix products, arithmetic and copies ran while one was open for 40% of the time, Pallas kernels for 0%

commit v1 on v0

v1 whole, which is shorter than its diff:
```python
import math

import jax
import jax.numpy as jnp
from jax import lax
from jax.experimental import pallas as pl
from jax.experimental.pallas import tpu as pltpu
from jax.sharding import Mesh
from jax.sharding import PartitionSpec as P

HD = 128
SPAN = 64
NBT = 128
NEIGH = 2
STEP_SPANS = 2

LOW = jnp.bfloat16
F32 = jnp.float32


def dot_nt(a, b):
    return lax.dot_general(a, b, (((1,), (1,)), ((), ())), preferred_element_type=F32)


def dot_tn(a, b):
    return lax.dot_general(a, b, (((0,), (0,)), ((), ())), preferred_element_type=F32)


def dot_nn(a, b):
    return lax.dot_general(a, b, (((1,), (0,)), ((), ())), preferred_element_type=F32)


def attention_kernel(heads, owners, ids, place, q_ref, g_ref, k_ref, v_ref, dq_ref, store_ref, total):
    step = pl.program_id(0)
    factor = 1.0 / math.sqrt(HD)
    width = heads * HD
    me = lax.axis_index("enc")

    @pl.when(step == 0)
    def _():
        total[...] = jnp.zeros_like(total)

    for s in range(STEP_SPANS):
        span = step * STEP_SPANS + s
        slots = []
        for j in range(NEIGH):
            entry = place[0, ids[span, j]]
            away = jnp.where(me % 2 == 0, entry // 2 - me, me - entry // 2)
            slots.append(lax.rem(away + owners, owners) * 2 + entry % 2)
        for h in range(heads):
            cols = slice(h * HD, (h + 1) * HD)
            rows = slice(s * SPAN, (s + 1) * SPAN)
            q = q_ref[rows, cols]
            g = g_ref[rows, cols]
            k = k_ref[s * NEIGH : (s + 1) * NEIGH, :, cols].reshape(NEIGH * NBT, HD)
            v = v_ref[s * NEIGH : (s + 1) * NEIGH, :, cols].reshape(NEIGH * NBT, HD)
            scores = dot_nt(q, k) * factor
            weight_grad = dot_nt(g, v)
            exponent = jnp.exp(scores - jnp.max(scores, axis=1, keepdims=True))
            weights = exponent * (1.0 / jnp.sum(exponent, axis=1, keepdims=True))
            weights_low = weights.astype(LOW)
            delta = jnp.sum(weights_low.astype(F32) * weight_grad, axis=1, keepdims=True)
            score_low = (weights * (weight_grad - delta)).astype(LOW)
            dq_ref[rows, cols] = (dot_nn(score_low, k) * factor).astype(LOW)
            key_grad = dot_tn(score_low, q)
            value_grad = dot_tn(weights_low, g)
            for j in range(NEIGH):
                part = slice(j * NBT, (j + 1) * NBT)
                total[slots[j], :, cols] += key_grad[part]
                total[slots[j], :, width + h * HD : width + (h + 1) * HD] += value_grad[part]

    @pl.when(step == pl.num_programs(0) - 1)
    def _():
        store_ref[:, :, :width] = (total[:, :, :width] * factor).astype(LOW)
        store_ref[:, :, width:] = total[:, :, width:].astype(LOW)


def attention(queries, out_grad, keys, values, ids, place, owners):
    tokens, width = queries.shape
    slots = keys.shape[0]
    entries = place.shape[1]
    steps = slots // (NEIGH * STEP_SPANS)
    row_spec = pl.BlockSpec((STEP_SPANS * SPAN, width), lambda i: (i, 0))
    slot_spec = pl.BlockSpec((STEP_SPANS * NEIGH, NBT, width), lambda i: (i, 0, 0))
    scalars = pl.BlockSpec(memory_space=pltpu.SMEM)

    def kernel(*refs):
        attention_kernel(width // HD, owners, *refs)

    return pl.pallas_call(
        kernel,
        grid=(steps,),
        in_specs=[scalars, scalars, row_spec, row_spec, slot_spec, slot_spec],
        out_specs=[row_spec, pl.BlockSpec((entries, NBT, 2 * width), lambda i: (0, 0, 0))],
        out_shape=[
            jax.ShapeDtypeStruct((tokens, width), LOW),
            jax.ShapeDtypeStruct((entries, NBT, 2 * width), LOW),
        ],
        scratch_shapes=[pltpu.VMEM((entries, NBT, 2 * width), F32)],
        compiler_params=pltpu.CompilerParams(
            dimension_semantics=("arbitrary",), vmem_limit_bytes=40 * 1024 * 1024
        ),
        cost_estimate=pl.CostEstimate(flops=10**9, bytes_accessed=6 * 10**6, transcendentals=2 * 10**6),
        name="attention_back",
    )(ids, place, queries, out_grad, keys, values)


def gather_rows(mine, dp_count, x_count):
    rows, depth = mine.shape
    sources = dp_count * x_count
    copies = jnp.broadcast_to(mine[None], (sources, rows, depth))
    same = lax.all_to_all(copies, ("dp", "sx"), split_axis=0, concat_axis=0, tiled=True)
    other = lax.ppermute(same, "core", [(0, 1), (1, 0)])
    first = lax.axis_index("core") == 0
    low = jnp.where(first, same, other)
    high = jnp.where(first, other, same)
    return jnp.stack([low, high], axis=1).reshape(sources * 2 * rows, depth)


def add_low(a, b):
    return (a.astype(F32) + b.astype(F32)).astype(LOW)


def local(queries, out_grad, keys, values, neighbour_ids, neighbour_place, kv_weight):
    owners = lax.axis_size("enc")
    dp_count, x_count = lax.axis_size("dp"), lax.axis_size("sx")
    rows = kv_weight.shape[1]
    depth = 2 * kv_weight.shape[2]
    half = owners // 2
    opposite = [(i, (i + half) % owners) for i in range(owners)]
    even = [(i, i ^ 1) for i in range(owners)]
    odd = [(i, (i + 1) % owners if i % 2 else (i - 1) % owners) for i in range(owners)]

    mine = jnp.transpose(kv_weight, (1, 0, 2)).reshape(rows, depth)
    weight = gather_rows(mine, dp_count, x_count)
    query_grad, store = attention(
        queries, out_grad, keys, values, neighbour_ids, neighbour_place, owners
    )
    cap = store.shape[0] // owners
    chunk = cap * NBT

    def raw(j):
        return store[j * cap : (j + 1) * cap].reshape(chunk, depth)

    far_raw = lax.ppermute(raw(half), "enc", opposite)
    far_mine = lax.ppermute(mine, "enc", opposite)
    far_mine, weight = lax.optimization_barrier((far_mine, weight))
    far_weight = gather_rows(far_mine, dp_count, x_count)

    part = {j: dot_nt(raw(j), weight).astype(LOW) for j in range(owners) if j != half}

    def on_even(x):
        return lax.ppermute(x, "enc", even)

    def on_odd(x):
        return lax.ppermute(x, "enc", odd)

    a, b = on_even(part[half - 1]), on_odd(part[half + 1])
    for j in range(half - 2, 0, -1):
        a, b = on_even(add_low(b, part[j])), on_odd(add_low(a, part[owners - j]))
    encoded = (
        dot_nt(far_raw, far_weight)
        + part[0].astype(F32)
        + a.astype(F32)
        + b.astype(F32)
    )
    return (query_grad, encoded.astype(LOW).reshape(cap, NBT, -1))


def solution(mesh):
    devices = mesh.devices
    dp_count, seq_count, enc_count = devices.shape
    split = Mesh(
        devices.reshape(dp_count, seq_count // 2, 2, enc_count), ("dp", "sx", "core", "enc")
    )
    group = ("dp", "sx", "core")
    placed = (
        P(group, "enc"),
        P(group, "enc"),
        P(group, None, "enc"),
        P(group, None, "enc"),
        P(group, None),
        P(group, None),
        P(None, group, "enc"),
    )
    return jax.shard_map(
        local,
        mesh=split,
        in_specs=placed,
        out_specs=(P(group, "enc"), P(("dp", "sx", "core", "enc"), None, None)),
        check_vma=False,
    )
```

time: 155 us -> 121 us (0.78)
  starting transfers between devices: 4.02 us -> 40.4 us
  local copies, waits for them, and re-layouts: 43.1 us -> 9.73 us
  waiting for transfers between devices: 47.5 us -> 17.4 us
  blocking collectives: 15.9 us -> 29.8 us
  between operations: 14.1 us -> 0.88 us
  matrix products: 24.3 us -> 11.8 us
  Pallas kernels: 0 us -> 10.1 us
  other arithmetic: 4.9 us -> 0.4 us
    all_gather x1 -> x0, waiting for transfers between devices: 47.5 us -> none  [local(): piece = lax.all_gather(columns, ('dp', 'seq'), axis=1, tiled=True)]
    ppermute x0 -> x10, starting transfers between devices: none -> 36 us  [the longest x2 9.04 us: gather_rows(): other = lax.ppermute(same, 'core', [(0, 1), (1, 0)])]
    all_to_all x0 -> x1, blocking collectives: none -> 29.8 us  [gather_rows(): lax.all_to_all(copies, ('dp', 'sx'), split_axis=0, concat_axis=0, tiled=T...]
    all_gather x1 -> x0, local copies, waits for them, and re-layouts: 18.8 us -> none  [local(): piece = lax.all_gather(columns, ('dp', 'seq'), axis=1, tiled=True)]
    ppermute x0 -> x10, waiting for transfers between devices: none -> 17.4 us  [the longest x3 14.5 us: on_even(): return lax.ppermute(x, 'enc', even)]
    all_gather x1 -> x0, blocking collectives: 15.9 us -> none  [local(): columns = lax.all_gather(kv_weight, 'enc', axis=2, tiled=True)]
    dot_general x8, matrix products: 24.3 us -> 11.8 us  [dot_nt(): lax.dot_general(a, b, (((1,), (1,)), ((), ())), preferred_element_type=F32)]
    pallas_call x0 -> x1, Pallas kernels: none -> 10.1 us  [attention(): pl.pallas_call(kernel, grid=(steps,), in_specs=[scalars, scalars, row_spe...]
  transfers between devices with their start and end apart: 2 -> 11, of which waited for: 1 -> 3; matrix products, arithmetic and copies ran while one was open for 40% -> 10% of each run, Pallas kernels for 0% -> 8%
where the time goes in v1:
time: 121 us; the launch traced here: 120 us
  starting transfers between devices  40.4 us (33%)
  blocking collectives  29.8 us (25%)
  waiting for transfers between devices  17.4 us (14%)
  matrix products  11.8 us (10%)
  Pallas kernels  10.1 us (8%)
  local copies, waits for them, and re-layouts  9.73 us (8%)
    all_to_all x1, blocking collectives, gather_rows(): lax.all_to_all(copies, ('dp', 'sx'), split_axis=0, concat_axis=0, tiled=T...  29.8 us
    ppermute x3, waiting for transfers between devices, on_even(): return lax.ppermute(x, 'enc', even)  14.5 us
    dot_general x8, matrix products, dot_nt(): lax.dot_general(a, b, (((1,), (1,)), ((), ())), preferred_element_type=F32)  11.8 us
    pallas_call x1, Pallas kernels, attention(): pl.pallas_call(kernel, grid=(steps,), in_specs=[scalars, scalars, row_spe...  10.1 us
    ppermute x2, starting transfers between devices, gather_rows(): other = lax.ppermute(same, 'core', [(0, 1), (1, 0)])  9.04 us
    ppermute x3, starting transfers between devices, on_even(): return lax.ppermute(x, 'enc', even)  7.78 us
    ppermute x3, starting transfers between devices, on_odd(): return lax.ppermute(x, 'enc', odd)  7.54 us
    ppermute x1, starting transfers between devices, local(): far_mine = lax.ppermute(mine, 'enc', opposite)  7.45 us
  transfers between devices with their start and end apart: 11, of which 3 were waited for; matrix products, arithmetic and copies ran while one was open for 10% of the time, Pallas kernels for 8%

profile of v1, /device:TPU:1, one launch (start us, length us, event | category | flops | bytes accessed | tf_op | source)
XLA Modules:
  0.0 120.4 jit_solution(15996397781086423384)
XLA Ops:
  0.6 0.7 pad.4
  1.4 29.8 %all_to_all.10 = bf16[32,14,512]{2,1,0:T(8,128)(2,1)S(1)} all-to-all(bf16[32,14,512]{2,1,0:T(8,128)(2,1)S(1)} %broadcast_in_dim.4), channel_id=1, replica_groups=mesh['dp'=8,'sx'=4,'core'=2,'enc'=8] {'dp','sx'}, dimensions={0} | all-to-all | bytes 917504 | tf_op jit(solution)/shard_map/all_to_all | solution.py:112
  31.2 4.3 %collective-permute-start.2 = (bf16[32,14,512]{2,1,0:T(8,128)(2,1)S(1)}, bf16[32,14,512]{2,1,0:T(8,128)(2,1)S(1)}, u32[]{:S(2)}, u32[]{:S(2)}) collective-permute-start(bf16[32,14,512]{2,1,0:T(8,128)(2,1)S(1)} %all_to_all.10), channel_id=1, source_target_pairs={{0,8},{8,0},{1,9},{9,1},{2,10},{10,2},{3,11},{11,3},{4,12},{12,4},... | collective-permute-start | bytes 1376264 | tf_op jit(solution)/shard_map/ppermute | solution.py:113
  35.5 7.5 %collective-permute-start.1 = (bf16[14,512]{1,0:T(8,128)(2,1)S(1)}, bf16[14,512]{1,0:T(8,128)(2,1)}, u32[]{:S(2)}, u32[]{:S(2)}) collective-permute-start(bf16[14,512]{1,0:T(8,128)(2,1)S(1)} %bitcast.48), channel_id=1, source_target_pairs={{0,4},{1,5},{2,6},{3,7},{4,0},{5,1},{6,2},{7,3},{8,12},{9,13},{10,... | collective-permute-start | bytes 43016 | tf_op jit(solution)/shard_map/ppermute | solution.py:146
  43.0 0.8 copy.10.refs_0_
  43.7 1.2 %copy-done = bf16[16,128,256]{2,1,0:T(8,128)(2,1)S(1)} copy-done((bf16[16,128,256]{2,1,0:T(8,128)(2,1)S(1)}, bf16[16,128,256]{2,1,0:T(8,128)(2,1)}, u32[]{:S(2)}) %copy-start) | copy-done | bytes 1048600
  45.0 1.2 %copy-done.1 = bf16[16,128,256]{2,1,0:T(8,128)(2,1)S(1)} copy-done((bf16[16,128,256]{2,1,0:T(8,128)(2,1)S(1)}, bf16[16,128,256]{2,1,0:T(8,128)(2,1)}, u32[]{:S(2)}) %copy-start.1) | copy-done | bytes 1048600
  46.2 0.9 copy-done.2
  47.1 0.9 copy-done.3
  48.1 0.7 copy-done.4
  48.7 10.1 %attention_back.1 = (bf16[512,256]{1,0:T(8,128)(2,1)}, bf16[16,128,512]{2,1,0:T(8,128)(2,1)S(1)}) custom-call(s32[8,2]{1,0:T(8,128)S(1)} %copy.10.refs_0_, s32[1,16]{1,0:T(1,128)S(1)} %copy-done.4, bf16[512,256]{1,0:T(8,128)(2,1)S(1)} %copy-done.2, bf16[512,256]{1,0:T(8,128)(2,1)S(1)} %copy-done.3, bf16[16,128,256]{2,1,0:T(8,128)(2,1)S(1)} %copy-done, ...), custom_call_target="tpu_custom_call" | custom-call | flops 1000000000 | bytes 6000000 | tf_op jit(solution)/shard_map/attention_back/pallas_call | solution.py:90
  58.8 1.0 fusion.8
  60.4 1.2 %convolution_convert_fusion.5 = bf16[256,896]{1,0:T(8,128)(2,1)} fusion(bf16[256,512]{1,0:T(8,128)(2,1)S(1)} %bitcast.40, bf16[896,512]{1,0:T(8,128)(2,1)S(1)} %reshape.44), kind=kOutput, calls=%fused_computation.12 | convolution fusion | flops 235110400 | bytes 1638400 | tf_op jit(solution)/shard_map/dot_general | solution.py:22
  61.7 2.3 %collective-permute-start.4 = (bf16[256,896]{1,0:T(8,128)(2,1)}, bf16[256,896]{1,0:T(8,128)(2,1)}, u32[]{:S(2)}, u32[]{:S(2)}) collective-permute-start(bf16[256,896]{1,0:T(8,128)(2,1)} %convolution_convert_fusion.5), channel_id=1, source_target_pairs={{0,1},{1,0},{2,3},{3,2},{4,5},{5,4},{6,7},{7,6},{8,9},{9,8},{10,11... | collective-permute-start | bytes 1376264 | tf_op jit(solution)/shard_map/ppermute | solution.py:153
  64.0 0.5 convolution_convert_fusion.2
  64.4 1.9 %collective-permute-start.7 = (bf16[256,896]{1,0:T(8,128)(2,1)S(1)}, bf16[256,896]{1,0:T(8,128)(2,1)}, u32[]{:S(2)}, u32[]{:S(2)}) collective-permute-start(bf16[256,896]{1,0:T(8,128)(2,1)S(1)} %convolution_convert_fusion.2), channel_id=1, source_target_pairs={{0,7},{1,2},{2,1},{3,4},{4,3},{5,6},{6,5},{7,0},{8,15},{9,10},{10,... | collective-permute-start | bytes 1376264 | tf_op jit(solution)/shard_map/ppermute | solution.py:156
  66.4 1.6 %broadcast_in_dim.5 = bf16[32,14,512]{2,1,0:T(8,128)(2,1)} broadcast(bf16[14,512]{1,0:T(8,128)(2,1)} %collective-permute-done.1), dimensions={1,2} | broadcast | bytes 473088 | tf_op jit(solution)/shard_map/broadcast_in_dim | solution.py:111
  67.9 4.4 %all-to-all-start.1 = ((bf16[32,14,512]{2,1,0:T(8,128)(2,1)}), bf16[32,14,512]{2,1,0:T(8,128)(2,1)S(1)}, u32[]{:S(2)}, u32[]{:S(2)}) async-start(bf16[32,14,512]{2,1,0:T(8,128)(2,1)} %broadcast_in_dim.5), calls=%async_computation.1 | async-start | bytes 1048576 | tf_op jit(solution)/shard_map/all_to_all | solution.py:112
  72.4 3.3 %collective-permute-done.4 = bf16[256,896]{1,0:T(8,128)(2,1)} collective-permute-done((bf16[256,896]{1,0:T(8,128)(2,1)}, bf16[256,896]{1,0:T(8,128)(2,1)}, u32[]{:S(2)}, u32[]{:S(2)}) %collective-permute-start.4) | collective-permute-done | bytes 458784 | tf_op jit(solution)/shard_map/ppermute | solution.py:153
  75.7 2.3 %add_convert_fusion.3 = bf16[256,896]{1,0:T(8,128)(2,1)} fusion(bf16[256,896]{1,0:T(8,128)(2,1)} %collective-permute-done.4, bf16[256,512]{1,0:T(8,128)(2,1)S(1)} %bitcast.45, bf16[896,512]{1,0:T(8,128)(2,1)S(1)} %reshape.44), kind=kOutput, calls=%fused_computation.21 | convolution fusion | flops 236027904 | bytes 2097152 | tf_op jit(solution)/shard_map/dot_general | solution.py:22
  77.9 2.1 %collective-permute-start.5 = (bf16[256,896]{1,0:T(8,128)(2,1)}, bf16[256,896]{1,0:T(8,128)(2,1)}, u32[]{:S(2)}, u32[]{:S(2)}) collective-permute-start(bf16[256,896]{1,0:T(8,128)(2,1)} %add_convert_fusion.3), channel_id=1, source_target_pairs={{0,7},{1,2},{2,1},{3,4},{4,3},{5,6},{6,5},{7,0},{8,15},{9,10},{10,... | collective-permute-start | bytes 1376264 | tf_op jit(solution)/shard_map/ppermute | solution.py:156
  80.0 1.5 %add_convert_fusion.1 = bf16[256,896]{1,0:T(8,128)(2,1)S(1)} fusion(bf16[256,896]{1,0:T(8,128)(2,1)} %collective-permute-done.7, bf16[256,512]{1,0:T(8,128)(2,1)S(1)} %bitcast.44, bf16[896,512]{1,0:T(8,128)(2,1)S(1)} %reshape.44), kind=kOutput, calls=%fused_computation.19 | convolution fusion | flops 236027904 | bytes 2097152 | tf_op jit(solution)/shard_map/dot_general | solution.py:22
  81.5 2.5 %collective-permute-start.8 = (bf16[256,896]{1,0:T(8,128)(2,1)S(1)}, bf16[256,896]{1,0:T(8,128)(2,1)S(1)}, u32[]{:S(2)}, u32[]{:S(2)}) collective-permute-start(bf16[256,896]{1,0:T(8,128)(2,1)S(1)} %add_convert_fusion.1), channel_id=1, source_target_pairs={{0,1},{1,0},{2,3},{3,2},{4,5},{5,4},{6,7},{7,6},{8,9},{9,8},{10,11... | collective-permute-start | bytes 1376264 | tf_op jit(solution)/shard_map/ppermute | solution.py:153
  84.1 4.1 %collective-permute-start = (bf16[256,512]{1,0:T(8,128)(2,1)}, bf16[256,512]{1,0:T(8,128)(2,1)}, u32[]{:S(2)}, u32[]{:S(2)}) collective-permute-start(bf16[256,512]{1,0:T(8,128)(2,1)} %bitcast), channel_id=1, source_target_pairs={{0,4},{1,5},{2,6},{3,7},{4,0},{5,1},{6,2},{7,3},{8,12},{9,13},{10,... | collective-permute-start | bytes 786440 | tf_op jit(solution)/shard_map/ppermute | solution.py:145
  88.2 4.7 %collective-permute-start.3 = (bf16[32,14,512]{2,1,0:T(8,128)(2,1)S(1)}, bf16[32,14,512]{2,1,0:T(8,128)(2,1)S(1)}, u32[]{:S(2)}, u32[]{:S(2)}) collective-permute-start(bf16[32,14,512]{2,1,0:T(8,128)(2,1)S(1)} %all-to-all-done.1), channel_id=1, source_target_pairs={{0,8},{8,0},{1,9},{9,1},{2,10},{10,2},{3,11},{11,3},{4,12},{12,4},... | collective-permute-start | bytes 1376264 | tf_op jit(solution)/shard_map/ppermute | solution.py:113
  93.0 2.3 %add_convert_fusion.2 = bf16[256,896]{1,0:T(8,128)(2,1)} fusion(bf16[256,896]{1,0:T(8,128)(2,1)} %collective-permute-done.5, bf16[256,512]{1,0:T(8,128)(2,1)S(1)} %bitcast.43, bf16[896,512]{1,0:T(8,128)(2,1)S(1)} %reshape.44), kind=kOutput, calls=%fused_computation.20 | convolution fusion | flops 236027904 | bytes 2097152 | tf_op jit(solution)/shard_map/dot_general | solution.py:22
  95.2 3.0 %collective-permute-start.6 = (bf16[256,896]{1,0:T(8,128)(2,1)}, bf16[256,896]{1,0:T(8,128)(2,1)S(1)}, u32[]{:S(2)}, u32[]{:S(2)}) collective-permute-start(bf16[256,896]{1,0:T(8,128)(2,1)} %add_convert_fusion.2), channel_id=1, source_target_pairs={{0,1},{1,0},{2,3},{3,2},{4,5},{5,4},{6,7},{7,6},{8,9},{9,8},{10,11... | collective-permute-start | bytes 1376264 | tf_op jit(solution)/shard_map/ppermute | solution.py:153
  98.2 1.2 %add_convert_fusion = bf16[256,896]{1,0:T(8,128)(2,1)} fusion(bf16[256,896]{1,0:T(8,128)(2,1)S(1)} %collective-permute-done.8, bf16[256,512]{1,0:T(8,128)(2,1)S(1)} %bitcast.42, bf16[896,512]{1,0:T(8,128)(2,1)S(1)} %reshape.44), kind=kOutput, calls=%fused_computation.18 | convolution fusion | flops 236027904 | bytes 2097152 | tf_op jit(solution)/shard_map/dot_general | solution.py:22
  99.5 3.6 %collective-permute-start.9 = (bf16[256,896]{1,0:T(8,128)(2,1)}, bf16[256,896]{1,0:T(8,128)(2,1)}, u32[]{:S(2)}, u32[]{:S(2)}) collective-permute-start(bf16[256,896]{1,0:T(8,128)(2,1)} %add_convert_fusion), channel_id=1, source_target_pairs={{0,7},{1,2},{2,1},{3,4},{4,3},{5,6},{6,5},{7,0},{8,15},{9,10},{10,... | collective-permute-start | bytes 1376264 | tf_op jit(solution)/shard_map/ppermute | solution.py:156
  104.0 11.2 %collective-permute-done.6 = bf16[256,896]{1,0:T(8,128)(2,1)S(1)} collective-permute-done((bf16[256,896]{1,0:T(8,128)(2,1)}, bf16[256,896]{1,0:T(8,128)(2,1)S(1)}, u32[]{:S(2)}, u32[]{:S(2)}) %collective-permute-start.6) | collective-permute-done | bytes 458784 | tf_op jit(solution)/shard_map/ppermute | solution.py:153
  115.2 2.8 %collective-permute-done.9 = bf16[256,896]{1,0:T(8,128)(2,1)} collective-permute-done((bf16[256,896]{1,0:T(8,128)(2,1)}, bf16[256,896]{1,0:T(8,128)(2,1)}, u32[]{:S(2)}, u32[]{:S(2)}) %collective-permute-start.9) | collective-permute-done | bytes 458784 | tf_op jit(solution)/shard_map/ppermute | solution.py:156
  118.0 2.4 %fusion.7 = bf16[256,896]{1,0:T(8,128)(2,1)} fusion(f32[256,896]{1,0:T(8,128)S(1)} %fusion.6, bf16[256,512]{1,0:T(8,128)(2,1)} %collective-permute-done, bf16[896,512]{1,0:T(8,128)(2,1)S(1)} %reshape.45, bf16[256,896]{1,0:T(8,128)(2,1)} %collective-permute-done.9, bf16[256,896]{1,0:T(8,128)(2,1)S(1)} %collective-permute-done.6), kind=kOutput, calls=%fused_computation.15 | convolution fusion | flops 236257280 | bytes 3473408 | tf_op jit(solution)/shard_map/dot_general | solution.py:22
  (25 shorter events, 1.6 us)
Async XLA Ops:
  31.2 28.6 %collective-permute-start.2 = (bf16[32,14,512]{2,1,0:T(8,128)(2,1)S(1)}, bf16[32,14,512]{2,1,0:T(8,128)(2,1)S(1)}, u32[]{:S(2)}, u32[]{:S(2)}) collective-permute-start(bf16[32,14,512]{2,1,0:T(8,128)(2,1)S(1)} %all_to_all.10), channel_id=1, source_target_pairs={{0,8},{8,0},{1,9},{9,1},{2,10},{10,2},{3,11},{11,3},{4,12},{12,4},... | collective-permute-start | bytes 1376264 | tf_op jit(solution)/shard_map/ppermute | solution.py:113
  35.5 24.9 %collective-permute-start.1 = (bf16[14,512]{1,0:T(8,128)(2,1)S(1)}, bf16[14,512]{1,0:T(8,128)(2,1)}, u32[]{:S(2)}, u32[]{:S(2)}) collective-permute-start(bf16[14,512]{1,0:T(8,128)(2,1)S(1)} %bitcast.48), channel_id=1, source_target_pairs={{0,4},{1,5},{2,6},{3,7},{4,0},{5,1},{6,2},{7,3},{8,12},{9,13},{10,... | collective-permute-start | bytes 43016 | tf_op jit(solution)/shard_map/ppermute | solution.py:146
  43.7 1.2 %copy-start = (bf16[16,128,256]{2,1,0:T(8,128)(2,1)S(1)}, bf16[16,128,256]{2,1,0:T(8,128)(2,1)}, u32[]{:S(2)}) copy-start(bf16[16,128,256]{2,1,0:T(8,128)(2,1)} %refs_4_.1) | copy-start | bytes 3145732
  45.0 1.2 %copy-start.1 = (bf16[16,128,256]{2,1,0:T(8,128)(2,1)S(1)}, bf16[16,128,256]{2,1,0:T(8,128)(2,1)}, u32[]{:S(2)}) copy-start(bf16[16,128,256]{2,1,0:T(8,128)(2,1)} %refs_5_.1) | copy-start | bytes 3145732
  46.2 0.9 copy-start.2
  47.1 0.9 copy-start.3
  48.1 0.7 copy-start.4
  60.4 15.3 %copy-start.5 = (bf16[2,128,512]{2,1,0:T(8,128)(2,1)S(1)}, bf16[2,128,512]{2,1,0:T(8,128)(2,1)}, u32[]{:S(2)}) copy-start(bf16[2,128,512]{2,1,0:T(8,128)(2,1)} %get-tuple-element.15) | copy-start | bytes 786436
  61.7 14.0 %collective-permute-start.4 = (bf16[256,896]{1,0:T(8,128)(2,1)}, bf16[256,896]{1,0:T(8,128)(2,1)}, u32[]{:S(2)}, u32[]{:S(2)}) collective-permute-start(bf16[256,896]{1,0:T(8,128)(2,1)} %convolution_convert_fusion.5), channel_id=1, source_target_pairs={{0,1},{1,0},{2,3},{3,2},{4,5},{5,4},{6,7},{7,6},{8,9},{9,8},{10,11... | collective-permute-start | bytes 1376264 | tf_op jit(solution)/shard_map/ppermute | solution.py:153
  64.4 15.6 %collective-permute-start.7 = (bf16[256,896]{1,0:T(8,128)(2,1)S(1)}, bf16[256,896]{1,0:T(8,128)(2,1)}, u32[]{:S(2)}, u32[]{:S(2)}) collective-permute-start(bf16[256,896]{1,0:T(8,128)(2,1)S(1)} %convolution_convert_fusion.2), channel_id=1, source_target_pairs={{0,7},{1,2},{2,1},{3,4},{4,3},{5,6},{6,5},{7,0},{8,15},{9,10},{10,... | collective-permute-start | bytes 1376264 | tf_op jit(solution)/shard_map/ppermute | solution.py:156
  67.9 20.3 %all-to-all-start.1 = ((bf16[32,14,512]{2,1,0:T(8,128)(2,1)}), bf16[32,14,512]{2,1,0:T(8,128)(2,1)S(1)}, u32[]{:S(2)}, u32[]{:S(2)}) async-start(bf16[32,14,512]{2,1,0:T(8,128)(2,1)} %broadcast_in_dim.5), calls=%async_computation.1 | async-start | bytes 1048576 | tf_op jit(solution)/shard_map/all_to_all | solution.py:112
  77.9 15.0 %collective-permute-start.5 = (bf16[256,896]{1,0:T(8,128)(2,1)}, bf16[256,896]{1,0:T(8,128)(2,1)}, u32[]{:S(2)}, u32[]{:S(2)}) collective-permute-start(bf16[256,896]{1,0:T(8,128)(2,1)} %add_convert_fusion.3), channel_id=1, source_target_pairs={{0,7},{1,2},{2,1},{3,4},{4,3},{5,6},{6,5},{7,0},{8,15},{9,10},{10,... | collective-permute-start | bytes 1376264 | tf_op jit(solution)/shard_map/ppermute | solution.py:156
  81.5 16.7 %collective-permute-start.8 = (bf16[256,896]{1,0:T(8,128)(2,1)S(1)}, bf16[256,896]{1,0:T(8,128)(2,1)S(1)}, u32[]{:S(2)}, u32[]{:S(2)}) collective-permute-start(bf16[256,896]{1,0:T(8,128)(2,1)S(1)} %add_convert_fusion.1), channel_id=1, source_target_pairs={{0,1},{1,0},{2,3},{3,2},{4,5},{5,4},{6,7},{7,6},{8,9},{9,8},{10,11... | collective-permute-start | bytes 1376264 | tf_op jit(solution)/shard_map/ppermute | solution.py:153
  84.1 19.9 %collective-permute-start = (bf16[256,512]{1,0:T(8,128)(2,1)}, bf16[256,512]{1,0:T(8,128)(2,1)}, u32[]{:S(2)}, u32[]{:S(2)}) collective-permute-start(bf16[256,512]{1,0:T(8,128)(2,1)} %bitcast), channel_id=1, source_target_pairs={{0,4},{1,5},{2,6},{3,7},{4,0},{5,1},{6,2},{7,3},{8,12},{9,13},{10,... | collective-permute-start | bytes 786440 | tf_op jit(solution)/shard_map/ppermute | solution.py:145
  88.2 15.3 %collective-permute-start.3 = (bf16[32,14,512]{2,1,0:T(8,128)(2,1)S(1)}, bf16[32,14,512]{2,1,0:T(8,128)(2,1)S(1)}, u32[]{:S(2)}, u32[]{:S(2)}) collective-permute-start(bf16[32,14,512]{2,1,0:T(8,128)(2,1)S(1)} %all-to-all-done.1), channel_id=1, source_target_pairs={{0,8},{8,0},{1,9},{9,1},{2,10},{10,2},{3,11},{11,3},{4,12},{12,4},... | collective-permute-start | bytes 1376264 | tf_op jit(solution)/shard_map/ppermute | solution.py:113
  95.2 20.0 %collective-permute-start.6 = (bf16[256,896]{1,0:T(8,128)(2,1)}, bf16[256,896]{1,0:T(8,128)(2,1)S(1)}, u32[]{:S(2)}, u32[]{:S(2)}) collective-permute-start(bf16[256,896]{1,0:T(8,128)(2,1)} %add_convert_fusion.2), channel_id=1, source_target_pairs={{0,1},{1,0},{2,3},{3,2},{4,5},{5,4},{6,7},{7,6},{8,9},{9,8},{10,11... | collective-permute-start | bytes 1376264 | tf_op jit(solution)/shard_map/ppermute | solution.py:153
  99.5 18.6 %collective-permute-start.9 = (bf16[256,896]{1,0:T(8,128)(2,1)}, bf16[256,896]{1,0:T(8,128)(2,1)}, u32[]{:S(2)}, u32[]{:S(2)}) collective-permute-start(bf16[256,896]{1,0:T(8,128)(2,1)} %add_convert_fusion), channel_id=1, source_target_pairs={{0,7},{1,2},{2,1},{3,4},{4,3},{5,6},{6,5},{7,0},{8,15},{9,10},{10,... | collective-permute-start | bytes 1376264 | tf_op jit(solution)/shard_map/ppermute | solution.py:156

commit v2 on v1

--- a/solution.py
+++ b/solution.py
@@ -98,23 +98,55 @@
         ],
         scratch_shapes=[pltpu.VMEM((entries, NBT, 2 * width), F32)],
         compiler_params=pltpu.CompilerParams(
-            dimension_semantics=("arbitrary",), vmem_limit_bytes=40 * 1024 * 1024
+            dimension_semantics=("arbitrary",), vmem_limit_bytes=56 * 1024 * 1024
         ),
         cost_estimate=pl.CostEstimate(flops=10**9, bytes_accessed=6 * 10**6, transcendentals=2 * 10**6),
         name="attention_back",
     )(ids, place, queries, out_grad, keys, values)
 
 
-def gather_rows(mine, dp_count, x_count):
-    rows, depth = mine.shape
-    sources = dp_count * x_count
-    copies = jnp.broadcast_to(mine[None], (sources, rows, depth))
-    same = lax.all_to_all(copies, ("dp", "sx"), split_axis=0, concat_axis=0, tiled=True)
+def copies_for(mine, sources):
+    return jnp.broadcast_to(mine[None], (sources,) + mine.shape)
+
+
+def exchange(copies):
+    return lax.all_to_all(copies, ("dp", "sx"), split_axis=0, concat_axis=0, tiled=True)
+
+
+def all_rows(same):
+    sources, rows, depth = same.shape
     other = lax.ppermute(same, "core", [(0, 1), (1, 0)])
     first = lax.axis_index("core") == 0
     low = jnp.where(first, same, other)
     high = jnp.where(first, other, same)
     return jnp.stack([low, high], axis=1).reshape(sources * 2 * rows, depth)
+
+
+def project_kernel(store_ref, weight_ref, out_ref):
+    cap, tokens, depth = store_ref.shape
+    raw = store_ref[...].reshape(cap * tokens, depth)
+    out_ref[0] = dot_nt(raw, weight_ref[...]).astype(LOW)
+
+
+def project(store, weight, first, owners):
+    entries, tokens, depth = store.shape
+    cap = entries // owners
+    columns = weight.shape[0]
+    return pl.pallas_call(
+        project_kernel,
+        grid=(owners - 1,),
+        in_specs=[
+            pl.BlockSpec((cap, tokens, depth), lambda i: (lax.rem(i + first, owners), 0, 0)),
+            pl.BlockSpec((columns, depth), lambda i: (0, 0)),
+        ],
+        out_specs=pl.BlockSpec((1, cap * tokens, columns), lambda i: (i, 0, 0)),
+        out_shape=jax.ShapeDtypeStruct((owners - 1, cap * tokens, columns), LOW),
+        compiler_params=pltpu.CompilerParams(
+            dimension_semantics=("arbitrary",), vmem_limit_bytes=16 * 1024 * 1024
+        ),
+        cost_estimate=pl.CostEstimate(flops=8 * 10**9, bytes_accessed=3 * 10**7, transcendentals=0),
+        name="project",
+    )(store, weight)
 
 
 def add_low(a, b):
@@ -127,27 +159,23 @@
     rows = kv_weight.shape[1]
     depth = 2 * kv_weight.shape[2]
     half = owners // 2
-    opposite = [(i, (i + half) % owners) for i in range(owners)]
     even = [(i, i ^ 1) for i in range(owners)]
     odd = [(i, (i + 1) % owners if i % 2 else (i - 1) % owners) for i in range(owners)]
 
+    sources = dp_count * x_count
+
     mine = jnp.transpose(kv_weight, (1, 0, 2)).reshape(rows, depth)
-    weight = gather_rows(mine, dp_count, x_count)
+    same = exchange(copies_for(mine, sources))
     query_grad, store = attention(
         queries, out_grad, keys, values, neighbour_ids, neighbour_place, owners
     )
     cap = store.shape[0] // owners
-    chunk = cap * NBT
-
-    def raw(j):
-        return store[j * cap : (j + 1) * cap].reshape(chunk, depth)
-
-    far_raw = lax.ppermute(raw(half), "enc", opposite)
-    far_mine = lax.ppermute(mine, "enc", opposite)
-    far_mine, weight = lax.optimization_barrier((far_mine, weight))
-    far_weight = gather_rows(far_mine, dp_count, x_count)
-
-    part = {j: dot_nt(raw(j), weight).astype(LOW) for j in range(owners) if j != half}
+    same, store = lax.optimization_barrier((same, store))
+    weight = all_rows(same)
+
+    far = dot_nt(store[half * cap : (half + 1) * cap].reshape(cap * NBT, depth), weight).astype(LOW)
+    far, weight = lax.optimization_barrier((far, weight))
+    part = project(store, weight, half + 1, owners)
 
     def on_even(x):
         return lax.ppermute(x, "enc", even)
@@ -155,15 +183,18 @@
     def on_odd(x):
         return lax.ppermute(x, "enc", odd)
 
-    a, b = on_even(part[half - 1]), on_odd(part[half + 1])
+    cut = cap * NBT // 2
+    a, b = on_even(far[:cut]), on_odd(far[cut:])
+    forth, back = part[owners - 2], part[0]
+    forth = jnp.concatenate([forth[:cut], add_low(forth[cut:], b)], axis=0)
+    back = jnp.concatenate([add_low(back[:cut], a), back[cut:]], axis=0)
+    a, b = on_even(forth), on_odd(back)
     for j in range(half - 2, 0, -1):
-        a, b = on_even(add_low(b, part[j])), on_odd(add_low(a, part[owners - j]))
-    encoded = (
-        dot_nt(far_raw, far_weight)
-        + part[0].astype(F32)
-        + a.astype(F32)
-        + b.astype(F32)
-    )
+        a, b = (
+            on_even(add_low(b, part[half - 1 + j])),
+            on_odd(add_low(a, part[half - 1 - j])),
+        )
+    encoded = part[half - 1].astype(F32) + a.astype(F32) + b.astype(F32)
     return (query_grad, encoded.astype(LOW).reshape(cap, NBT, -1))
 
 

time: 121 us -> 106 us (0.88)
  the two profiles are of different devices: /device:TPU:1 before, /device:TPU:2 now
where the time goes in v2:
time: 106 us; the launch traced here: 105 us
  starting transfers between devices  41 us (39%)
  waiting for transfers between devices  40.1 us (38%)
  Pallas kernels  14.7 us (14%)
  local copies, waits for them, and re-layouts  5.37 us (5%)
  other arithmetic  2.74 us (3%)
    ppermute x4, waiting for transfers between devices, on_odd(): return lax.ppermute(x, 'enc', odd)  23.5 us
    ppermute x4, starting transfers between devices, on_odd(): return lax.ppermute(x, 'enc', odd)  16.3 us
    all_to_all x1, starting transfers between devices, exchange(): lax.all_to_all(copies, ('dp', 'sx'), split_axis=0, concat_axis=0, tiled=T...  13.5 us
    ppermute x4, waiting for transfers between devices, on_even(): return lax.ppermute(x, 'enc', even)  11.6 us
    pallas_call x1, Pallas kernels, attention(): pl.pallas_call(kernel, grid=(steps,), in_specs=[scalars, scalars, row_spe...  11.4 us
    ppermute x4, starting transfers between devices, on_even(): return lax.ppermute(x, 'enc', even)  9.3 us
    all_to_all x1, waiting for transfers between devices, exchange(): lax.all_to_all(copies, ('dp', 'sx'), split_axis=0, concat_axis=0, tiled=T...  4.1 us
    pallas_call x1, Pallas kernels, project(): pl.pallas_call(project_kernel, grid=(owners - 1,), in_specs=[pl.BlockSpec...  3.32 us
  transfers between devices with their start and end apart: 10, of which 10 were waited for; matrix products, arithmetic and copies ran while one was open for 2% of the time, Pallas kernels for 11%

profile of v2, /device:TPU:2, one launch (start us, length us, event | category | flops | bytes accessed | tf_op | source)
XLA Modules:
  0.0 105.2 jit_solution(18423929416250952085)
XLA Ops:
  0.6 0.7 pad.6
  1.4 0.9 broadcast_in_dim.8
  2.2 13.5 %all-to-all-start = ((bf16[32,14,512]{2,1,0:T(8,128)(2,1)}), bf16[32,14,512]{2,1,0:T(8,128)(2,1)S(1)}, u32[]{:S(2)}, u32[]{:S(2)}) async-start(bf16[32,14,512]{2,1,0:T(8,128)(2,1)} %broadcast_in_dim.8), calls=%async_computation | async-start | bytes 1048576 | tf_op jit(solution)/shard_map/all_to_all | solution.py:113
  15.7 1.3 %copy.11.refs_0_ = s32[8,2]{1,0:T(8,128)} copy(s32[8,2]{0,1:T(2,128)} %param.11) | data formatting | bytes 128 | tf_op args[4]
  17.1 11.4 %attention_back.1 = (bf16[512,256]{1,0:T(8,128)(2,1)}, bf16[16,128,512]{2,1,0:T(8,128)(2,1)}) custom-call(s32[8,2]{1,0:T(8,128)} %copy.11.refs_0_, s32[1,16]{1,0:T(1,128)} %refs_1_.1, bf16[512,256]{1,0:T(8,128)(2,1)} %refs_2_.1, bf16[512,256]{1,0:T(8,128)(2,1)} %refs_3_.1, bf16[16,128,256]{2,1,0:T(8,128)(2,1)} %refs_4_.1, bf16[16,128,256]{2,1,0:T(8,128)(2,1)} %refs_5_.1), custom_call_target="tpu_custom_call" | custom-call | flops 1000000000 | bytes 6000000 | tf_op jit(solution)/shard_map/attention_back/pallas_call | solution.py:90
  28.4 4.1 %all-to-all-done = bf16[32,14,512]{2,1,0:T(8,128)(2,1)S(1)} async-done(((bf16[32,14,512]{2,1,0:T(8,128)(2,1)}), bf16[32,14,512]{2,1,0:T(8,128)(2,1)S(1)}, u32[]{:S(2)}, u32[]{:S(2)}) %all-to-all-start) | async-done | bytes 458784 | tf_op jit(solution)/shard_map/all_to_all | solution.py:113
  32.5 1.9 %collective-permute-start = (bf16[32,14,512]{2,1,0:T(8,128)(2,1)S(1)}, bf16[32,14,512]{2,1,0:T(8,128)(2,1)S(1)}, u32[]{:S(2)}, u32[]{:S(2)}) collective-permute-start(bf16[32,14,512]{2,1,0:T(8,128)(2,1)S(1)} %all-to-all-done), channel_id=1, source_target_pairs={{0,8},{8,0},{1,9},{9,1},{2,10},{10,2},{3,11},{11,3},{4,12},{12,4},... | collective-permute-start | bytes 1376264 | tf_op jit(solution)/shard_map/ppermute | solution.py:118
  34.5 1.0 slice.50
  35.4 0.9 collective-permute-done
  36.4 1.1 %pad_maximum_fusion = bf16[32,2,14,512]{3,2,1,0:T(8,128)(2,1)} fusion(bf16[32,1,14,512]{3,2,1,0:T(8,128)(2,1)S(1)} %get-tuple-element.23, bf16[32,1,14,512]{3,2,1,0:T(8,128)(2,1)S(1)} %get-tuple-element.22), kind=kLoop, calls=%fused_computation.1 | loop fusion | flops 458752 | bytes 1835008 | tf_op jit(solution)/shard_map/stack | solution.py:122
  37.5 1.4 %reshape.33.weight_ref = bf16[896,512]{1,0:T(8,128)(2,1)S(1)} reshape(bf16[32,2,14,512]{3,2,1,0:T(8,128)(2,1)} %pad_maximum_fusion) | data formatting | bytes 1835008 | tf_op jit(solution)/shard_map/reshape | solution.py:122
  38.9 0.5 convolution_convert_fusion
  39.4 3.3 %project.1 = bf16[7,256,896]{2,1,0:T(8,128)(2,1)S(1)} custom-call(bf16[16,128,512]{2,1,0:T(8,128)(2,1)S(1)} %copy-done, bf16[896,512]{1,0:T(8,128)(2,1)S(1)} %reshape.33.weight_ref), custom_call_target="tpu_custom_call" | custom-call | flops 8000000000 | bytes 30000000 | tf_op jit(solution)/shard_map/project/pallas_call | solution.py:135
  42.8 5.4 %collective-permute-start.1 = (bf16[128,896]{1,0:T(8,128)(2,1)S(1)}, bf16[128,896]{1,0:T(8,128)(2,1)S(1)}, u32[]{:S(2)}, u32[]{:S(2)}) collective-permute-start(bf16[128,896]{1,0:T(8,128)(2,1)S(1)} %get-tuple-element.24), channel_id=1, source_target_pairs={{0,7},{1,2},{2,1},{3,4},{4,3},{5,6},{6,5},{7,0},{8,15},{9,10},{10,... | collective-permute-start | bytes 688136 | tf_op jit(solution)/shard_map/ppermute | solution.py:184
  48.1 1.9 %collective-permute-start.5 = (bf16[128,896]{1,0:T(8,128)(2,1)S(1)}, bf16[128,896]{1,0:T(8,128)(2,1)S(1)}, u32[]{:S(2)}, u32[]{:S(2)}) collective-permute-start(bf16[128,896]{1,0:T(8,128)(2,1)S(1)} %get-tuple-element.25), channel_id=1, source_target_pairs={{0,1},{1,0},{2,3},{3,2},{4,5},{5,4},{6,7},{7,6},{8,9},{9,8},{10,11... | collective-permute-start | bytes 688136 | tf_op jit(solution)/shard_map/ppermute | solution.py:181
  50.1 3.9 %collective-permute-done.1 = bf16[128,896]{1,0:T(8,128)(2,1)S(1)} collective-permute-done((bf16[128,896]{1,0:T(8,128)(2,1)S(1)}, bf16[128,896]{1,0:T(8,128)(2,1)S(1)}, u32[]{:S(2)}, u32[]{:S(2)}) %collective-permute-start.1) | collective-permute-done | bytes 229408 | tf_op jit(solution)/shard_map/ppermute | solution.py:184
  54.0 3.4 %collective-permute-done.5 = bf16[128,896]{1,0:T(8,128)(2,1)S(1)} collective-permute-done((bf16[128,896]{1,0:T(8,128)(2,1)S(1)}, bf16[128,896]{1,0:T(8,128)(2,1)S(1)}, u32[]{:S(2)}, u32[]{:S(2)}) %collective-permute-start.5) | collective-permute-done | bytes 229408 | tf_op jit(solution)/shard_map/ppermute | solution.py:181
  57.6 2.9 %collective-permute-start.6 = (bf16[256,896]{1,0:T(8,128)(2,1)S(1)}, bf16[256,896]{1,0:T(8,128)(2,1)S(1)}, u32[]{:S(2)}, u32[]{:S(2)}) collective-permute-start(bf16[256,896]{1,0:T(8,128)(2,1)S(1)} %pad_maximum_fusion.2), channel_id=1, source_target_pairs={{0,7},{1,2},{2,1},{3,4},{4,3},{5,6},{6,5},{7,0},{8,15},{9,10},{10,... | collective-permute-start | bytes 1376264 | tf_op jit(solution)/shard_map/ppermute | solution.py:184
  60.5 3.3 %collective-permute-start.2 = (bf16[256,896]{1,0:T(8,128)(2,1)S(1)}, bf16[256,896]{1,0:T(8,128)(2,1)S(1)}, u32[]{:S(2)}, u32[]{:S(2)}) collective-permute-start(bf16[256,896]{1,0:T(8,128)(2,1)S(1)} %pad_maximum_fusion.1), channel_id=1, source_target_pairs={{0,1},{1,0},{2,3},{3,2},{4,5},{5,4},{6,7},{7,6},{8,9},{9,8},{10,11... | collective-permute-start | bytes 1376264 | tf_op jit(solution)/shard_map/ppermute | solution.py:181
  63.8 8.3 %collective-permute-done.6 = bf16[256,896]{1,0:T(8,128)(2,1)S(1)} collective-permute-done((bf16[256,896]{1,0:T(8,128)(2,1)S(1)}, bf16[256,896]{1,0:T(8,128)(2,1)S(1)}, u32[]{:S(2)}, u32[]{:S(2)}) %collective-permute-start.6) | collective-permute-done | bytes 458784 | tf_op jit(solution)/shard_map/ppermute | solution.py:184
  72.1 1.8 %collective-permute-done.2 = bf16[256,896]{1,0:T(8,128)(2,1)S(1)} collective-permute-done((bf16[256,896]{1,0:T(8,128)(2,1)S(1)}, bf16[256,896]{1,0:T(8,128)(2,1)S(1)}, u32[]{:S(2)}, u32[]{:S(2)}) %collective-permute-start.2) | collective-permute-done | bytes 458784 | tf_op jit(solution)/shard_map/ppermute | solution.py:181
  73.8 0.2 fusion.3
  74.1 3.9 %collective-permute-start.3 = (bf16[256,896]{1,0:T(8,128)(2,1)S(1)}, bf16[256,896]{1,0:T(8,128)(2,1)S(1)}, u32[]{:S(2)}, u32[]{:S(2)}) collective-permute-start(bf16[256,896]{1,0:T(8,128)(2,1)S(1)} %get-tuple-element.16), channel_id=1, source_target_pairs={{0,7},{1,2},{2,1},{3,4},{4,3},{5,6},{6,5},{7,0},{8,15},{9,10},{10,... | collective-permute-start | bytes 1376264 | tf_op jit(solution)/shard_map/ppermute | solution.py:184
  77.9 1.9 %collective-permute-start.7 = (bf16[256,896]{1,0:T(8,128)(2,1)S(1)}, bf16[256,896]{1,0:T(8,128)(2,1)S(1)}, u32[]{:S(2)}, u32[]{:S(2)}) collective-permute-start(bf16[256,896]{1,0:T(8,128)(2,1)S(1)} %get-tuple-element.17), channel_id=1, source_target_pairs={{0,1},{1,0},{2,3},{3,2},{4,5},{5,4},{6,7},{7,6},{8,9},{9,8},{10,11... | collective-permute-start | bytes 1376264 | tf_op jit(solution)/shard_map/ppermute | solution.py:181
  79.9 7.8 %collective-permute-done.3 = bf16[256,896]{1,0:T(8,128)(2,1)S(1)} collective-permute-done((bf16[256,896]{1,0:T(8,128)(2,1)S(1)}, bf16[256,896]{1,0:T(8,128)(2,1)S(1)}, u32[]{:S(2)}, u32[]{:S(2)}) %collective-permute-start.3) | collective-permute-done | bytes 458784 | tf_op jit(solution)/shard_map/ppermute | solution.py:184
  87.7 2.0 %collective-permute-done.7 = bf16[256,896]{1,0:T(8,128)(2,1)S(1)} collective-permute-done((bf16[256,896]{1,0:T(8,128)(2,1)S(1)}, bf16[256,896]{1,0:T(8,128)(2,1)S(1)}, u32[]{:S(2)}, u32[]{:S(2)}) %collective-permute-start.7) | collective-permute-done | bytes 458784 | tf_op jit(solution)/shard_map/ppermute | solution.py:181
  89.7 0.2 fusion.2
  90.0 2.2 %collective-permute-start.4 = (bf16[256,896]{1,0:T(8,128)(2,1)S(1)}, bf16[256,896]{1,0:T(8,128)(2,1)S(1)}, u32[]{:S(2)}, u32[]{:S(2)}) collective-permute-start(bf16[256,896]{1,0:T(8,128)(2,1)S(1)} %get-tuple-element.14), channel_id=1, source_target_pairs={{0,1},{1,0},{2,3},{3,2},{4,5},{5,4},{6,7},{7,6},{8,9},{9,8},{10,11... | collective-permute-start | bytes 1376264 | tf_op jit(solution)/shard_map/ppermute | solution.py:181
  92.2 4.2 %collective-permute-start.8 = (bf16[256,896]{1,0:T(8,128)(2,1)S(1)}, bf16[256,896]{1,0:T(8,128)(2,1)S(1)}, u32[]{:S(2)}, u32[]{:S(2)}) collective-permute-start(bf16[256,896]{1,0:T(8,128)(2,1)S(1)} %get-tuple-element.15), channel_id=1, source_target_pairs={{0,7},{1,2},{2,1},{3,4},{4,3},{5,6},{6,5},{7,0},{8,15},{9,10},{10,... | collective-permute-start | bytes 1376264 | tf_op jit(solution)/shard_map/ppermute | solution.py:184
  96.4 4.4 %collective-permute-done.4 = bf16[256,896]{1,0:T(8,128)(2,1)S(1)} collective-permute-done((bf16[256,896]{1,0:T(8,128)(2,1)S(1)}, bf16[256,896]{1,0:T(8,128)(2,1)S(1)}, u32[]{:S(2)}, u32[]{:S(2)}) %collective-permute-start.4) | collective-permute-done | bytes 458784 | tf_op jit(solution)/shard_map/ppermute | solution.py:181
  100.9 3.4 %collective-permute-done.8 = bf16[256,896]{1,0:T(8,128)(2,1)S(1)} collective-permute-done((bf16[256,896]{1,0:T(8,128)(2,1)S(1)}, bf16[256,896]{1,0:T(8,128)(2,1)S(1)}, u32[]{:S(2)}, u32[]{:S(2)}) %collective-permute-start.8) | collective-permute-done | bytes 458784 | tf_op jit(solution)/shard_map/ppermute | solution.py:184
  104.3 0.9 fusion.5
  (9 shorter events, 0.4 us)
Async XLA Ops:
  2.2 30.3 %all-to-all-start = ((bf16[32,14,512]{2,1,0:T(8,128)(2,1)}), bf16[32,14,512]{2,1,0:T(8,128)(2,1)S(1)}, u32[]{:S(2)}, u32[]{:S(2)}) async-start(bf16[32,14,512]{2,1,0:T(8,128)(2,1)} %broadcast_in_dim.8), calls=%async_computation | async-start | bytes 1048576 | tf_op jit(solution)/shard_map/all_to_all | solution.py:113
  32.5 3.8 %collective-permute-start = (bf16[32,14,512]{2,1,0:T(8,128)(2,1)S(1)}, bf16[32,14,512]{2,1,0:T(8,128)(2,1)S(1)}, u32[]{:S(2)}, u32[]{:S(2)}) collective-permute-start(bf16[32,14,512]{2,1,0:T(8,128)(2,1)S(1)} %all-to-all-done), channel_id=1, source_target_pairs={{0,8},{8,0},{1,9},{9,1},{2,10},{10,2},{3,11},{11,3},{4,12},{12,4},... | collective-permute-start | bytes 1376264 | tf_op jit(solution)/shard_map/ppermute | solution.py:118
  36.4 3.0 %copy-start = (bf16[16,128,512]{2,1,0:T(8,128)(2,1)S(1)}, bf16[16,128,512]{2,1,0:T(8,128)(2,1)}, u32[]{:S(2)}) copy-start(bf16[16,128,512]{2,1,0:T(8,128)(2,1)} %get-tuple-element.10.store_ref) | copy-start | bytes 6291460
  42.8 11.3 %collective-permute-start.1 = (bf16[128,896]{1,0:T(8,128)(2,1)S(1)}, bf16[128,896]{1,0:T(8,128)(2,1)S(1)}, u32[]{:S(2)}, u32[]{:S(2)}) collective-permute-start(bf16[128,896]{1,0:T(8,128)(2,1)S(1)} %get-tuple-element.24), channel_id=1, source_target_pairs={{0,7},{1,2},{2,1},{3,4},{4,3},{5,6},{6,5},{7,0},{8,15},{9,10},{10,... | collective-permute-start | bytes 688136 | tf_op jit(solution)/shard_map/ppermute | solution.py:184
  48.1 9.3 %collective-permute-start.5 = (bf16[128,896]{1,0:T(8,128)(2,1)S(1)}, bf16[128,896]{1,0:T(8,128)(2,1)S(1)}, u32[]{:S(2)}, u32[]{:S(2)}) collective-permute-start(bf16[128,896]{1,0:T(8,128)(2,1)S(1)} %get-tuple-element.25), channel_id=1, source_target_pairs={{0,1},{1,0},{2,3},{3,2},{4,5},{5,4},{6,7},{7,6},{8,9},{9,8},{10,11... | collective-permute-start | bytes 688136 | tf_op jit(solution)/shard_map/ppermute | solution.py:181
  57.6 14.5 %collective-permute-start.6 = (bf16[256,896]{1,0:T(8,128)(2,1)S(1)}, bf16[256,896]{1,0:T(8,128)(2,1)S(1)}, u32[]{:S(2)}, u32[]{:S(2)}) collective-permute-start(bf16[256,896]{1,0:T(8,128)(2,1)S(1)} %pad_maximum_fusion.2), channel_id=1, source_target_pairs={{0,7},{1,2},{2,1},{3,4},{4,3},{5,6},{6,5},{7,0},{8,15},{9,10},{10,... | collective-permute-start | bytes 1376264 | tf_op jit(solution)/shard_map/ppermute | solution.py:184
  60.5 13.3 %collective-permute-start.2 = (bf16[256,896]{1,0:T(8,128)(2,1)S(1)}, bf16[256,896]{1,0:T(8,128)(2,1)S(1)}, u32[]{:S(2)}, u32[]{:S(2)}) collective-permute-start(bf16[256,896]{1,0:T(8,128)(2,1)S(1)} %pad_maximum_fusion.1), channel_id=1, source_target_pairs={{0,1},{1,0},{2,3},{3,2},{4,5},{5,4},{6,7},{7,6},{8,9},{9,8},{10,11... | collective-permute-start | bytes 1376264 | tf_op jit(solution)/shard_map/ppermute | solution.py:181
  74.1 13.6 %collective-permute-start.3 = (bf16[256,896]{1,0:T(8,128)(2,1)S(1)}, bf16[256,896]{1,0:T(8,128)(2,1)S(1)}, u32[]{:S(2)}, u32[]{:S(2)}) collective-permute-start(bf16[256,896]{1,0:T(8,128)(2,1)S(1)} %get-tuple-element.16), channel_id=1, source_target_pairs={{0,7},{1,2},{2,1},{3,4},{4,3},{5,6},{6,5},{7,0},{8,15},{9,10},{10,... | collective-permute-start | bytes 1376264 | tf_op jit(solution)/shard_map/ppermute | solution.py:184
  77.9 11.8 %collective-permute-start.7 = (bf16[256,896]{1,0:T(8,128)(2,1)S(1)}, bf16[256,896]{1,0:T(8,128)(2,1)S(1)}, u32[]{:S(2)}, u32[]{:S(2)}) collective-permute-start(bf16[256,896]{1,0:T(8,128)(2,1)S(1)} %get-tuple-element.17), channel_id=1, source_target_pairs={{0,1},{1,0},{2,3},{3,2},{4,5},{5,4},{6,7},{7,6},{8,9},{9,8},{10,11... | collective-permute-start | bytes 1376264 | tf_op jit(solution)/shard_map/ppermute | solution.py:181
  90.0 10.9 %collective-permute-start.4 = (bf16[256,896]{1,0:T(8,128)(2,1)S(1)}, bf16[256,896]{1,0:T(8,128)(2,1)S(1)}, u32[]{:S(2)}, u32[]{:S(2)}) collective-permute-start(bf16[256,896]{1,0:T(8,128)(2,1)S(1)} %get-tuple-element.14), channel_id=1, source_target_pairs={{0,1},{1,0},{2,3},{3,2},{4,5},{5,4},{6,7},{7,6},{8,9},{9,8},{10,11... | collective-permute-start | bytes 1376264 | tf_op jit(solution)/shard_map/ppermute | solution.py:181
  92.2 12.1 %collective-permute-start.8 = (bf16[256,896]{1,0:T(8,128)(2,1)S(1)}, bf16[256,896]{1,0:T(8,128)(2,1)S(1)}, u32[]{:S(2)}, u32[]{:S(2)}) collective-permute-start(bf16[256,896]{1,0:T(8,128)(2,1)S(1)} %get-tuple-element.15), channel_id=1, source_target_pairs={{0,7},{1,2},{2,1},{3,4},{4,3},{5,6},{6,5},{7,0},{8,15},{9,10},{10,... | collective-permute-start | bytes 1376264 | tf_op jit(solution)/shard_map/ppermute | solution.py:184

commit v3 on v1

v3 whole, which is shorter than its diff:
```python
import math

import jax
import jax.numpy as jnp
from jax import lax
from jax.experimental import pallas as pl
from jax.experimental.pallas import tpu as pltpu
from jax.sharding import Mesh
from jax.sharding import PartitionSpec as P

HD = 128
SPAN = 64
NBT = 128
NEIGH = 2
STEP_SPANS = 4

LOW = jnp.bfloat16
F32 = jnp.float32


def dot_nt(a, b):
    return lax.dot_general(a, b, (((1,), (1,)), ((), ())), preferred_element_type=F32)


def dot_tn(a, b):
    return lax.dot_general(a, b, (((0,), (0,)), ((), ())), preferred_element_type=F32)


def dot_nn(a, b):
    return lax.dot_general(a, b, (((1,), (0,)), ((), ())), preferred_element_type=F32)


def softmax_back(scores, weight_grad):
    exponent = jnp.exp(scores - jnp.max(scores, axis=1, keepdims=True))
    weights = exponent * (1.0 / jnp.sum(exponent, axis=1, keepdims=True))
    weights_low = weights.astype(LOW)
    delta = jnp.sum(weights_low.astype(F32) * weight_grad, axis=1, keepdims=True)
    return weights_low, (weights * (weight_grad - delta)).astype(LOW)


def attention_kernel(heads, owners, ids, place, q_ref, g_ref, k_ref, v_ref, dq_ref, store_ref, far_ref, total):
    step = pl.program_id(0)
    factor = 1.0 / math.sqrt(HD)
    width = heads * HD
    me = lax.axis_index("enc")

    @pl.when(step == 0)
    def _():
        total[...] = jnp.zeros_like(total)

    slots = []
    for s in range(STEP_SPANS):
        for j in range(NEIGH):
            entry = place[0, ids[j, step * STEP_SPANS + s]]
            away = jnp.where(me % 2 == 0, entry // 2 - me, me - entry // 2)
            slots.append(lax.rem(away + owners, owners) * 2 + entry % 2)

    def rows_of(ref, unit):
        s, h = unit
        return ref[s * SPAN : (s + 1) * SPAN, h * HD : (h + 1) * HD]

    def slots_of(ref, unit):
        s, h = unit
        block = ref[s * NEIGH : (s + 1) * NEIGH, :, h * HD : (h + 1) * HD]
        return block.reshape(NEIGH * NBT, HD)

    units = [(s, h) for s in range(STEP_SPANS) for h in range(heads)]
    scores = [dot_nt(rows_of(q_ref, u), slots_of(k_ref, u)) * factor for u in units]
    weight_grads = [dot_nt(rows_of(g_ref, u), slots_of(v_ref, u)) for u in units]
    lows = [softmax_back(a, b) for a, b in zip(scores, weight_grads)]
    for (s, h), (_, score_low) in zip(units, lows):
        dq = dot_nn(score_low, slots_of(k_ref, (s, h))) * factor
        dq_ref[s * SPAN : (s + 1) * SPAN, h * HD : (h + 1) * HD] = dq.astype(LOW)
    key_grads = [dot_tn(low[1], rows_of(q_ref, u)) for low, u in zip(lows, units)]
    value_grads = [dot_tn(low[0], rows_of(g_ref, u)) for low, u in zip(lows, units)]
    for (s, h), key_grad, value_grad in zip(units, key_grads, value_grads):
        for j in range(NEIGH):
            slot = slots[s * NEIGH + j]
            part = slice(j * NBT, (j + 1) * NBT)
            total[slot, :, h * HD : (h + 1) * HD] += key_grad[part]
            total[slot, :, width + h * HD : width + (h + 1) * HD] += value_grad[part]

    @pl.when(step == pl.num_programs(0) - 1)
    def _():
        store_ref[:, :, :width] = (total[:, :, :width] * factor).astype(LOW)
        store_ref[:, :, width:] = total[:, :, width:].astype(LOW)
        far_ref[...] = store_ref[pl.ds(store_ref.shape[0] // 2, far_ref.shape[0])]


def attention(queries, out_grad, keys, values, ids, place, owners):
    tokens, width = queries.shape
    slots = keys.shape[0]
    entries = place.shape[1]
    steps = slots // (NEIGH * STEP_SPANS)
    row_spec = pl.BlockSpec((STEP_SPANS * SPAN, width), lambda i: (i, 0))
    slot_spec = pl.BlockSpec((STEP_SPANS * NEIGH, NBT, width), lambda i: (i, 0, 0))
    scalars = pl.BlockSpec(memory_space=pltpu.SMEM)

    def whole_spec(count):
        return pl.BlockSpec((count, NBT, 2 * width), lambda i: (0, 0, 0))

    def kernel(*refs):
        attention_kernel(width // HD, owners, *refs)

    return pl.pallas_call(
        kernel,
        grid=(steps,),
        in_specs=[scalars, scalars, row_spec, row_spec, slot_spec, slot_spec],
        out_specs=[row_spec, whole_spec(entries), whole_spec(entries // owners)],
        out_shape=[
            jax.ShapeDtypeStruct((tokens, width), LOW),
            jax.ShapeDtypeStruct((entries, NBT, 2 * width), LOW),
            jax.ShapeDtypeStruct((entries // owners, NBT, 2 * width), LOW),
        ],
        scratch_shapes=[pltpu.VMEM((entries, NBT, 2 * width), F32)],
        compiler_params=pltpu.CompilerParams(
            dimension_semantics=("arbitrary",), vmem_limit_bytes=56 * 1024 * 1024
        ),
        cost_estimate=pl.CostEstimate(flops=10**9, bytes_accessed=6 * 10**6, transcendentals=2 * 10**6),
        name="attention_back",
    )(ids.T, place, queries, out_grad, keys, values)


def exchange(mine):
    sources = lax.axis_size("dp") * lax.axis_size("sx")
    copies = jnp.broadcast_to(mine[None], (sources,) + mine.shape)
    return lax.all_to_all(copies, ("dp", "sx"), split_axis=0, concat_axis=0, tiled=True)


def all_rows(same):
    sources, rows, depth = same.shape
    other = lax.ppermute(same, "core", [(0, 1), (1, 0)])
    first = lax.axis_index("core") == 0
    low = jnp.where(first, same, other)
    high = jnp.where(first, other, same)
    return jnp.stack([low, high], axis=1).reshape(sources * 2 * rows, depth)


def add_low(a, b):
    return (a.astype(F32) + b.astype(F32)).astype(LOW)


def local(queries, out_grad, keys, values, neighbour_ids, neighbour_place, kv_weight):
    owners = lax.axis_size("enc")
    rows = kv_weight.shape[1]
    half = owners // 2
    even = [(i, i ^ 1) for i in range(owners)]
    odd = [(i, (i + 1) % owners if i % 2 else (i - 1) % owners) for i in range(owners)]

    same = exchange(jnp.transpose(kv_weight, (1, 0, 2)).reshape(rows, -1))
    query_grad, store, far_store = attention(
        queries, out_grad, keys, values, neighbour_ids, neighbour_place, owners
    )
    cap = store.shape[0] // owners
    same, store, far_store = lax.optimization_barrier((same, store, far_store))
    weight = all_rows(same)

    def project(raw, weight):
        raw = raw.reshape(cap * NBT, -1)
        return lax.optimization_barrier(dot_nt(raw, weight).astype(LOW))

    def chunk(j):
        return store[j * cap : (j + 1) * cap]

    def on_even(x):
        return lax.ppermute(x, "enc", even)

    def on_odd(x):
        return lax.ppermute(x, "enc", odd)

    cut = cap * NBT // 2
    far = project(far_store, weight)
    a, b = on_even(far[:cut]), on_odd(far[cut:])
    back, forth = project(chunk(half + 1), weight), project(chunk(half - 1), weight)
    weight, _ = lax.optimization_barrier((weight, a))
    back = jnp.concatenate([add_low(back[:cut], a), back[cut:]], axis=0)
    forth = jnp.concatenate([forth[:cut], add_low(forth[cut:], b)], axis=0)
    a, b = on_even(forth), on_odd(back)
    for j in range(half - 2, 0, -1):
        forth, back = project(chunk(j), weight), project(chunk(owners - j), weight)
        a, b = on_even(add_low(b, forth)), on_odd(add_low(a, back))
    own = project(chunk(0), weight)
    encoded = own.astype(F32) + a.astype(F32) + b.astype(F32)
    return (query_grad, encoded.astype(LOW).reshape(cap, NBT, -1))


def solution(mesh):
    devices = mesh.devices
    dp_count, seq_count, enc_count = devices.shape
    split = Mesh(
        devices.reshape(dp_count, seq_count // 2, 2, enc_count), ("dp", "sx", "core", "enc")
    )
    group = ("dp", "sx", "core")
    placed = (
        P(group, "enc"),
        P(group, "enc"),
        P(group, None, "enc"),
        P(group, None, "enc"),
        P(group, None),
        P(group, None),
        P(None, group, "enc"),
    )
    return jax.shard_map(
        local,
        mesh=split,
        in_specs=placed,
        out_specs=(P(group, "enc"), P(("dp", "sx", "core", "enc"), None, None)),
        check_vma=False,
    )
```

time: 121 us -> 96.9 us (0.80)
  the two profiles are of different devices: /device:TPU:1 before, /device:TPU:8 now
where the time goes in v3:
time: 96.9 us; the launch traced here: 96.3 us
  starting transfers between devices  45.8 us (47%)
  waiting for transfers between devices  32.9 us (34%)
  Pallas kernels  6 us (6%)
  matrix products  4.7 us (5%)
  local copies, waits for them, and re-layouts  4.26 us (4%)
  other arithmetic  1.76 us (2%)
    ppermute x4, starting transfers between devices, on_odd(): return lax.ppermute(x, 'enc', odd)  16.1 us
    ppermute x4, starting transfers between devices, on_even(): return lax.ppermute(x, 'enc', even)  14.6 us
    all_to_all x1, starting transfers between devices, exchange(): lax.all_to_all(copies, ('dp', 'sx'), split_axis=0, concat_axis=0, tiled=T...  13.2 us
    all_to_all x1, waiting for transfers between devices, exchange(): lax.all_to_all(copies, ('dp', 'sx'), split_axis=0, concat_axis=0, tiled=T...  11.7 us
    ppermute x4, waiting for transfers between devices, on_even(): return lax.ppermute(x, 'enc', even)  11.2 us
    ppermute x4, waiting for transfers between devices, on_odd(): return lax.ppermute(x, 'enc', odd)  9.93 us
    pallas_call x1, Pallas kernels, attention(): pl.pallas_call(kernel, grid=(steps,), in_specs=[scalars, scalars, row_spe...  6 us
    dot_general x8, matrix products, dot_nt(): lax.dot_general(a, b, (((1,), (1,)), ((), ())), preferred_element_type=F32)  4.7 us
  transfers between devices with their start and end apart: 10, of which 7 were waited for; matrix products, arithmetic and copies ran while one was open for 6% of the time, Pallas kernels for 6%

profile of v3, /device:TPU:8, one launch (start us, length us, event | category | flops | bytes accessed | tf_op | source)
XLA Modules:
  0.0 96.3 jit_solution(13608962252584382281)
XLA Ops:
  0.6 0.7 pad.6
  1.4 0.9 broadcast_in_dim.8
  2.2 13.2 %all-to-all-start = ((bf16[32,14,512]{2,1,0:T(8,128)(2,1)}), bf16[32,14,512]{2,1,0:T(8,128)(2,1)S(1)}, u32[]{:S(2)}, u32[]{:S(2)}) async-start(bf16[32,14,512]{2,1,0:T(8,128)(2,1)} %broadcast_in_dim.8), calls=%async_computation | async-start | bytes 1048576 | tf_op jit(solution)/shard_map/all_to_all | solution.py:127
  15.4 6.0 %attention_back.1 = (bf16[512,256]{1,0:T(8,128)(2,1)}, bf16[16,128,512]{2,1,0:T(8,128)(2,1)}, bf16[2,128,512]{2,1,0:T(8,128)(2,1)}) custom-call(s32[2,8]{1,0:T(2,128)} %bitcast.48, s32[1,16]{1,0:T(1,128)} %refs_1_.1, bf16[512,256]{1,0:T(8,128)(2,1)} %refs_2_.1, bf16[512,256]{1,0:T(8,128)(2,1)} %refs_3_.1, bf16[16,128,256]{2,1,0:T(8,128)(2,1)} %refs_4_.1, ...), custom_call_target="tpu_custom_call" | custom-call | flops 1000000000 | bytes 6000000 | tf_op jit(solution)/shard_map/attention_back/pallas_call | solution.py:105
  21.4 11.7 %all-to-all-done = bf16[32,14,512]{2,1,0:T(8,128)(2,1)S(1)} async-done(((bf16[32,14,512]{2,1,0:T(8,128)(2,1)}), bf16[32,14,512]{2,1,0:T(8,128)(2,1)S(1)}, u32[]{:S(2)}, u32[]{:S(2)}) %all-to-all-start) | async-done | bytes 458784 | tf_op jit(solution)/shard_map/all_to_all | solution.py:127
  33.1 1.9 %collective-permute-start = (bf16[32,14,512]{2,1,0:T(8,128)(2,1)S(1)}, bf16[32,14,512]{2,1,0:T(8,128)(2,1)S(1)}, u32[]{:S(2)}, u32[]{:S(2)}) collective-permute-start(bf16[32,14,512]{2,1,0:T(8,128)(2,1)S(1)} %all-to-all-done), channel_id=1, source_target_pairs={{0,8},{8,0},{1,9},{9,1},{2,10},{10,2},{3,11},{11,3},{4,12},{12,4},... | collective-permute-start | bytes 1376264 | tf_op jit(solution)/shard_map/ppermute | solution.py:132
  35.0 2.3 %fusion = (bf16[2,128,512]{2,1,0:T(8,128)(2,1)S(1)}, bf16[2,128,512]{2,1,0:T(8,128)(2,1)S(1)}, bf16[2,128,512]{2,1,0:T(8,128)(2,1)S(1)}, bf16[2,128,512]{2,1,0:T...) fusion(bf16[16,128,512]{2,1,0:T(8,128)(2,1)} %get-tuple-element.12), kind=kLoop, calls=%fused_computation.20 | loop fusion | bytes 3670016 | tf_op jit(solution)/shard_map/slice | solution.py:163
  37.4 0.1 pad_maximum_fusion
  37.6 0.3 reshape.36
  37.9 1.5 %convolution_convert_fusion.7 = bf16[256,896]{1,0:T(8,128)(2,1)S(1)} fusion(bf16[256,512]{1,0:T(8,128)(2,1)} %bitcast.44, bf16[896,512]{1,0:T(8,128)(2,1)S(1)} %reshape.36), kind=kOutput, calls=%fused_computation.7 | convolution fusion | flops 235110400 | bytes 1638400 | tf_op jit(solution)/shard_map/dot_general | solution.py:22
  39.4 2.4 %collective-permute-start.1 = (bf16[128,896]{1,0:T(8,128)(2,1)S(1)}, bf16[128,896]{1,0:T(8,128)(2,1)S(1)}, u32[]{:S(2)}, u32[]{:S(2)}) collective-permute-start(bf16[128,896]{1,0:T(8,128)(2,1)S(1)} %get-tuple-element.26), channel_id=1, source_target_pairs={{0,1},{1,0},{2,3},{3,2},{4,5},{5,4},{6,7},{7,6},{8,9},{9,8},{10,11... | collective-permute-start | bytes 688136 | tf_op jit(solution)/shard_map/ppermute | solution.py:166
  41.7 0.5 convolution_convert_fusion.2
  42.2 4.6 %collective-permute-start.2 = (bf16[128,896]{1,0:T(8,128)(2,1)S(1)}, bf16[128,896]{1,0:T(8,128)(2,1)S(1)}, u32[]{:S(2)}, u32[]{:S(2)}) collective-permute-start(bf16[128,896]{1,0:T(8,128)(2,1)S(1)} %get-tuple-element.25), channel_id=1, source_target_pairs={{0,7},{1,2},{2,1},{3,4},{4,3},{5,6},{6,5},{7,0},{8,15},{9,10},{10,... | collective-permute-start | bytes 688136 | tf_op jit(solution)/shard_map/ppermute | solution.py:169
  46.9 0.5 convolution_convert_fusion.5
  47.4 1.9 %collective-permute-done.1 = bf16[128,896]{1,0:T(8,128)(2,1)S(1)} collective-permute-done((bf16[128,896]{1,0:T(8,128)(2,1)S(1)}, bf16[128,896]{1,0:T(8,128)(2,1)S(1)}, u32[]{:S(2)}, u32[]{:S(2)}) %collective-permute-start.1) | collective-permute-done | bytes 229408 | tf_op jit(solution)/shard_map/ppermute | solution.py:166
  49.4 3.5 %collective-permute-start.6 = (bf16[256,896]{1,0:T(8,128)(2,1)S(1)}, bf16[256,896]{1,0:T(8,128)(2,1)S(1)}, u32[]{:S(2)}, u32[]{:S(2)}) collective-permute-start(bf16[256,896]{1,0:T(8,128)(2,1)S(1)} %pad_maximum_fusion.2), channel_id=1, source_target_pairs={{0,7},{1,2},{2,1},{3,4},{4,3},{5,6},{6,5},{7,0},{8,15},{9,10},{10,... | collective-permute-start | bytes 1376264 | tf_op jit(solution)/shard_map/ppermute | solution.py:169
  52.9 0.5 convolution_convert_fusion
  53.3 0.5 convolution_convert_fusion.1
  53.9 4.3 %collective-permute-start.3 = (bf16[256,896]{1,0:T(8,128)(2,1)S(1)}, bf16[256,896]{1,0:T(8,128)(2,1)S(1)}, u32[]{:S(2)}, u32[]{:S(2)}) collective-permute-start(bf16[256,896]{1,0:T(8,128)(2,1)S(1)} %pad_maximum_fusion.1), channel_id=1, source_target_pairs={{0,1},{1,0},{2,3},{3,2},{4,5},{5,4},{6,7},{7,6},{8,9},{9,8},{10,11... | collective-permute-start | bytes 1376264 | tf_op jit(solution)/shard_map/ppermute | solution.py:166
  58.2 0.5 convolution_convert_fusion.4
  58.7 4.7 %collective-permute-done.6 = bf16[256,896]{1,0:T(8,128)(2,1)S(1)} collective-permute-done((bf16[256,896]{1,0:T(8,128)(2,1)S(1)}, bf16[256,896]{1,0:T(8,128)(2,1)S(1)}, u32[]{:S(2)}, u32[]{:S(2)}) %collective-permute-start.6) | collective-permute-done | bytes 458784 | tf_op jit(solution)/shard_map/ppermute | solution.py:169
  63.5 4.1 %collective-permute-start.7 = (bf16[256,896]{1,0:T(8,128)(2,1)S(1)}, bf16[256,896]{1,0:T(8,128)(2,1)S(1)}, u32[]{:S(2)}, u32[]{:S(2)}) collective-permute-start(bf16[256,896]{1,0:T(8,128)(2,1)S(1)} %add_convert_fusion.2), channel_id=1, source_target_pairs={{0,1},{1,0},{2,3},{3,2},{4,5},{5,4},{6,7},{7,6},{8,9},{9,8},{10,11... | collective-permute-start | bytes 1376264 | tf_op jit(solution)/shard_map/ppermute | solution.py:166
  67.6 1.3 %collective-permute-done.3 = bf16[256,896]{1,0:T(8,128)(2,1)S(1)} collective-permute-done((bf16[256,896]{1,0:T(8,128)(2,1)S(1)}, bf16[256,896]{1,0:T(8,128)(2,1)S(1)}, u32[]{:S(2)}, u32[]{:S(2)}) %collective-permute-start.3) | collective-permute-done | bytes 458784 | tf_op jit(solution)/shard_map/ppermute | solution.py:166
  69.0 4.1 %collective-permute-start.4 = (bf16[256,896]{1,0:T(8,128)(2,1)S(1)}, bf16[256,896]{1,0:T(8,128)(2,1)S(1)}, u32[]{:S(2)}, u32[]{:S(2)}) collective-permute-start(bf16[256,896]{1,0:T(8,128)(2,1)S(1)} %add_convert_fusion.4), channel_id=1, source_target_pairs={{0,7},{1,2},{2,1},{3,4},{4,3},{5,6},{6,5},{7,0},{8,15},{9,10},{10,... | collective-permute-start | bytes 1376264 | tf_op jit(solution)/shard_map/ppermute | solution.py:169
  73.1 0.5 convolution_convert_fusion.3
  73.6 4.5 %collective-permute-done.7 = bf16[256,896]{1,0:T(8,128)(2,1)S(1)} collective-permute-done((bf16[256,896]{1,0:T(8,128)(2,1)S(1)}, bf16[256,896]{1,0:T(8,128)(2,1)S(1)}, u32[]{:S(2)}, u32[]{:S(2)}) %collective-permute-start.7) | collective-permute-done | bytes 458784 | tf_op jit(solution)/shard_map/ppermute | solution.py:166
  78.2 3.9 %collective-permute-start.8 = (bf16[256,896]{1,0:T(8,128)(2,1)S(1)}, bf16[256,896]{1,0:T(8,128)(2,1)S(1)}, u32[]{:S(2)}, u32[]{:S(2)}) collective-permute-start(bf16[256,896]{1,0:T(8,128)(2,1)S(1)} %add_convert_fusion.1), channel_id=1, source_target_pairs={{0,7},{1,2},{2,1},{3,4},{4,3},{5,6},{6,5},{7,0},{8,15},{9,10},{10,... | collective-permute-start | bytes 1376264 | tf_op jit(solution)/shard_map/ppermute | solution.py:169
  82.3 3.9 %collective-permute-start.5 = (bf16[256,896]{1,0:T(8,128)(2,1)S(1)}, bf16[256,896]{1,0:T(8,128)(2,1)S(1)}, u32[]{:S(2)}, u32[]{:S(2)}) collective-permute-start(bf16[256,896]{1,0:T(8,128)(2,1)S(1)} %add_convert_fusion.3), channel_id=1, source_target_pairs={{0,1},{1,0},{2,3},{3,2},{4,5},{5,4},{6,7},{7,6},{8,9},{9,8},{10,11... | collective-permute-start | bytes 1376264 | tf_op jit(solution)/shard_map/ppermute | solution.py:166
  86.2 0.5 convolution_convert_fusion.6
  86.7 5.2 %collective-permute-done.8 = bf16[256,896]{1,0:T(8,128)(2,1)S(1)} collective-permute-done((bf16[256,896]{1,0:T(8,128)(2,1)S(1)}, bf16[256,896]{1,0:T(8,128)(2,1)S(1)}, u32[]{:S(2)}, u32[]{:S(2)}) %collective-permute-start.8) | collective-permute-done | bytes 458784 | tf_op jit(solution)/shard_map/ppermute | solution.py:169
  91.9 3.5 %collective-permute-done.5 = bf16[256,896]{1,0:T(8,128)(2,1)S(1)} collective-permute-done((bf16[256,896]{1,0:T(8,128)(2,1)S(1)}, bf16[256,896]{1,0:T(8,128)(2,1)S(1)}, u32[]{:S(2)}, u32[]{:S(2)}) %collective-permute-start.5) | collective-permute-done | bytes 458784 | tf_op jit(solution)/shard_map/ppermute | solution.py:166
  95.4 0.9 add_convert_fusion
  (18 shorter events, 0.8 us)
Async XLA Ops:
  2.2 30.9 %all-to-all-start = ((bf16[32,14,512]{2,1,0:T(8,128)(2,1)}), bf16[32,14,512]{2,1,0:T(8,128)(2,1)S(1)}, u32[]{:S(2)}, u32[]{:S(2)}) async-start(bf16[32,14,512]{2,1,0:T(8,128)(2,1)} %broadcast_in_dim.8), calls=%async_computation | async-start | bytes 1048576 | tf_op jit(solution)/shard_map/all_to_all | solution.py:127
  33.1 4.2 %collective-permute-start = (bf16[32,14,512]{2,1,0:T(8,128)(2,1)S(1)}, bf16[32,14,512]{2,1,0:T(8,128)(2,1)S(1)}, u32[]{:S(2)}, u32[]{:S(2)}) collective-permute-start(bf16[32,14,512]{2,1,0:T(8,128)(2,1)S(1)} %all-to-all-done), channel_id=1, source_target_pairs={{0,8},{8,0},{1,9},{9,1},{2,10},{10,2},{3,11},{11,3},{4,12},{12,4},... | collective-permute-start | bytes 1376264 | tf_op jit(solution)/shard_map/ppermute | solution.py:132
  37.8 3.9 %copy-start = (bf16[2,128,512]{2,1,0:T(8,128)(2,1)S(1)}, bf16[2,128,512]{2,1,0:T(8,128)(2,1)}, u32[]{:S(2)}) copy-start(bf16[2,128,512]{2,1,0:T(8,128)(2,1)} %get-tuple-element.19) | copy-start | bytes 786436
  39.4 9.9 %collective-permute-start.1 = (bf16[128,896]{1,0:T(8,128)(2,1)S(1)}, bf16[128,896]{1,0:T(8,128)(2,1)S(1)}, u32[]{:S(2)}, u32[]{:S(2)}) collective-permute-start(bf16[128,896]{1,0:T(8,128)(2,1)S(1)} %get-tuple-element.26), channel_id=1, source_target_pairs={{0,1},{1,0},{2,3},{3,2},{4,5},{5,4},{6,7},{7,6},{8,9},{9,8},{10,11... | collective-permute-start | bytes 688136 | tf_op jit(solution)/shard_map/ppermute | solution.py:166
  42.2 11.6 %collective-permute-start.2 = (bf16[128,896]{1,0:T(8,128)(2,1)S(1)}, bf16[128,896]{1,0:T(8,128)(2,1)S(1)}, u32[]{:S(2)}, u32[]{:S(2)}) collective-permute-start(bf16[128,896]{1,0:T(8,128)(2,1)S(1)} %get-tuple-element.25), channel_id=1, source_target_pairs={{0,7},{1,2},{2,1},{3,4},{4,3},{5,6},{6,5},{7,0},{8,15},{9,10},{10,... | collective-permute-start | bytes 688136 | tf_op jit(solution)/shard_map/ppermute | solution.py:169
  49.4 14.0 %collective-permute-start.6 = (bf16[256,896]{1,0:T(8,128)(2,1)S(1)}, bf16[256,896]{1,0:T(8,128)(2,1)S(1)}, u32[]{:S(2)}, u32[]{:S(2)}) collective-permute-start(bf16[256,896]{1,0:T(8,128)(2,1)S(1)} %pad_maximum_fusion.2), channel_id=1, source_target_pairs={{0,7},{1,2},{2,1},{3,4},{4,3},{5,6},{6,5},{7,0},{8,15},{9,10},{10,... | collective-permute-start | bytes 1376264 | tf_op jit(solution)/shard_map/ppermute | solution.py:169
  53.9 15.0 %collective-permute-start.3 = (bf16[256,896]{1,0:T(8,128)(2,1)S(1)}, bf16[256,896]{1,0:T(8,128)(2,1)S(1)}, u32[]{:S(2)}, u32[]{:S(2)}) collective-permute-start(bf16[256,896]{1,0:T(8,128)(2,1)S(1)} %pad_maximum_fusion.1), channel_id=1, source_target_pairs={{0,1},{1,0},{2,3},{3,2},{4,5},{5,4},{6,7},{7,6},{8,9},{9,8},{10,11... | collective-permute-start | bytes 1376264 | tf_op jit(solution)/shard_map/ppermute | solution.py:166
  63.5 14.6 %collective-permute-start.7 = (bf16[256,896]{1,0:T(8,128)(2,1)S(1)}, bf16[256,896]{1,0:T(8,128)(2,1)S(1)}, u32[]{:S(2)}, u32[]{:S(2)}) collective-permute-start(bf16[256,896]{1,0:T(8,128)(2,1)S(1)} %add_convert_fusion.2), channel_id=1, source_target_pairs={{0,1},{1,0},{2,3},{3,2},{4,5},{5,4},{6,7},{7,6},{8,9},{9,8},{10,11... | collective-permute-start | bytes 1376264 | tf_op jit(solution)/shard_map/ppermute | solution.py:166
  69.0 13.2 %collective-permute-start.4 = (bf16[256,896]{1,0:T(8,128)(2,1)S(1)}, bf16[256,896]{1,0:T(8,128)(2,1)S(1)}, u32[]{:S(2)}, u32[]{:S(2)}) collective-permute-start(bf16[256,896]{1,0:T(8,128)(2,1)S(1)} %add_convert_fusion.4), channel_id=1, source_target_pairs={{0,7},{1,2},{2,1},{3,4},{4,3},{5,6},{6,5},{7,0},{8,15},{9,10},{10,... | collective-permute-start | bytes 1376264 | tf_op jit(solution)/shard_map/ppermute | solution.py:169
  78.2 13.6 %collective-permute-start.8 = (bf16[256,896]{1,0:T(8,128)(2,1)S(1)}, bf16[256,896]{1,0:T(8,128)(2,1)S(1)}, u32[]{:S(2)}, u32[]{:S(2)}) collective-permute-start(bf16[256,896]{1,0:T(8,128)(2,1)S(1)} %add_convert_fusion.1), channel_id=1, source_target_pairs={{0,7},{1,2},{2,1},{3,4},{4,3},{5,6},{6,5},{7,0},{8,15},{9,10},{10,... | collective-permute-start | bytes 1376264 | tf_op jit(solution)/shard_map/ppermute | solution.py:169
  82.3 13.1 %collective-permute-start.5 = (bf16[256,896]{1,0:T(8,128)(2,1)S(1)}, bf16[256,896]{1,0:T(8,128)(2,1)S(1)}, u32[]{:S(2)}, u32[]{:S(2)}) collective-permute-start(bf16[256,896]{1,0:T(8,128)(2,1)S(1)} %add_convert_fusion.3), channel_id=1, source_target_pairs={{0,1},{1,0},{2,3},{3,2},{4,5},{5,4},{6,7},{7,6},{8,9},{9,8},{10,11... | collective-permute-start | bytes 1376264 | tf_op jit(solution)/shard_map/ppermute | solution.py:166

commit v4 on v3

v4 whole, which is shorter than its diff:
```python
import math

import jax
import jax.numpy as jnp
from jax import lax
from jax.experimental import pallas as pl
from jax.experimental.pallas import tpu as pltpu
from jax.sharding import Mesh
from jax.sharding import PartitionSpec as P

HD = 128
SPAN = 64
NBT = 128
NEIGH = 2
STEP_SPANS = 4

LOW = jnp.bfloat16
F32 = jnp.float32


def dot_nt(a, b):
    return lax.dot_general(a, b, (((1,), (1,)), ((), ())), preferred_element_type=F32)


def dot_tn(a, b):
    return lax.dot_general(a, b, (((0,), (0,)), ((), ())), preferred_element_type=F32)


def dot_nn(a, b):
    return lax.dot_general(a, b, (((1,), (0,)), ((), ())), preferred_element_type=F32)


def softmax_back(scores, weight_grad):
    exponent = jnp.exp(scores - jnp.max(scores, axis=1, keepdims=True))
    weights = exponent * (1.0 / jnp.sum(exponent, axis=1, keepdims=True))
    weights_low = weights.astype(LOW)
    delta = jnp.sum(weights_low.astype(F32) * weight_grad, axis=1, keepdims=True)
    return weights_low, (weights * (weight_grad - delta)).astype(LOW)


def entry_place(me, entry, owners):
    owner = entry // 2
    pairs = owners // 2
    parity = owner % 2
    side = me % 2
    ahead = lax.rem(owner // 2 - me // 2 + pairs, pairs)
    near = (ahead == 1) | (ahead == pairs - 1)
    handler = jnp.where(near, jnp.where(ahead == 1, 1, 0), parity)
    slot = jnp.where(near, jnp.where(handler == parity, 2, 1), jnp.where(ahead == 0, 3, 0))
    return (jnp.where(handler == side, 0, pairs) + slot) * 2 + entry % 2


def attention_kernel(heads, owners, ids, place, q_ref, g_ref, k_ref, v_ref, dq_ref, kept_ref, *rest):
    *sent_refs, total = rest
    step = pl.program_id(0)
    factor = 1.0 / math.sqrt(HD)
    width = heads * HD
    me = lax.axis_index("pair") * 2 + lax.axis_index("side")

    @pl.when(step == 0)
    def _():
        total[...] = jnp.zeros_like(total)

    slots = []
    for s in range(STEP_SPANS):
        for j in range(NEIGH):
            entry = place[0, ids[j, step * STEP_SPANS + s]]
            slots.append(entry_place(me, entry, owners))

    def rows_of(ref, unit):
        s, h = unit
        return ref[s * SPAN : (s + 1) * SPAN, h * HD : (h + 1) * HD]

    def slots_of(ref, unit):
        s, h = unit
        block = ref[s * NEIGH : (s + 1) * NEIGH, :, h * HD : (h + 1) * HD]
        return block.reshape(NEIGH * NBT, HD)

    units = [(s, h) for s in range(STEP_SPANS) for h in range(heads)]
    scores = [dot_nt(rows_of(q_ref, u), slots_of(k_ref, u)) * factor for u in units]
    weight_grads = [dot_nt(rows_of(g_ref, u), slots_of(v_ref, u)) for u in units]
    lows = [softmax_back(a, b) for a, b in zip(scores, weight_grads)]
    for (s, h), (_, score_low) in zip(units, lows):
        dq = dot_nn(score_low, slots_of(k_ref, (s, h))) * factor
        dq_ref[s * SPAN : (s + 1) * SPAN, h * HD : (h + 1) * HD] = dq.astype(LOW)
    key_grads = [dot_tn(low[1], rows_of(q_ref, u)) for low, u in zip(lows, units)]
    value_grads = [dot_tn(low[0], rows_of(g_ref, u)) for low, u in zip(lows, units)]
    for (s, h), key_grad, value_grad in zip(units, key_grads, value_grads):
        for j in range(NEIGH):
            slot = slots[s * NEIGH + j]
            part = slice(j * NBT, (j + 1) * NBT)
            total[slot, :, h * HD : (h + 1) * HD] += key_grad[part]
            total[slot, :, width + h * HD : width + (h + 1) * HD] += value_grad[part]

    @pl.when(step == pl.num_programs(0) - 1)
    def _():
        first = 0
        for ref in (kept_ref, *sent_refs):
            part = slice(first, first + ref.shape[0])
            ref[:, :, :width] = (total[part, :, :width] * factor).astype(LOW)
            ref[:, :, width:] = total[part, :, width:].astype(LOW)
            first += ref.shape[0]


def attention(queries, out_grad, keys, values, ids, place, owners):
    tokens, width = queries.shape
    slots = keys.shape[0]
    entries = place.shape[1]
    steps = slots // (NEIGH * STEP_SPANS)
    row_spec = pl.BlockSpec((STEP_SPANS * SPAN, width), lambda i: (i, 0))
    slot_spec = pl.BlockSpec((STEP_SPANS * NEIGH, NBT, width), lambda i: (i, 0, 0))
    scalars = pl.BlockSpec(memory_space=pltpu.SMEM)

    shapes = [(entries // 2, NBT, 2 * width)] * 2

    def kernel(*refs):
        attention_kernel(width // HD, owners, *refs)

    return pl.pallas_call(
        kernel,
        grid=(steps,),
        in_specs=[scalars, scalars, row_spec, row_spec, slot_spec, slot_spec],
        out_specs=[row_spec] + [pl.BlockSpec(shape, lambda i: (0, 0, 0)) for shape in shapes],
        out_shape=[jax.ShapeDtypeStruct((tokens, width), LOW)]
        + [jax.ShapeDtypeStruct(shape, LOW) for shape in shapes],
        scratch_shapes=[pltpu.VMEM((entries, NBT, 2 * width), F32)],
        compiler_params=pltpu.CompilerParams(
            dimension_semantics=("arbitrary",), vmem_limit_bytes=56 * 1024 * 1024
        ),
        cost_estimate=pl.CostEstimate(flops=10**9, bytes_accessed=6 * 10**6, transcendentals=2 * 10**6),
        name="attention_back",
    )(ids.T, place, queries, out_grad, keys, values)


def exchange(mine, axes):
    sizes = tuple(lax.axis_size(axis) for axis in axes)
    copies = jnp.broadcast_to(mine[None], (math.prod(sizes),) + mine.shape)
    theirs = lax.all_to_all(copies, axes, split_axis=0, concat_axis=0, tiled=True)
    return theirs.reshape(sizes + mine.shape)


def column_order(rows):
    x_count, dp_count = lax.axis_size("sx"), lax.axis_size("dp")
    count = 2 * x_count * dp_count * rows
    at = jnp.arange(count, dtype=jnp.int32)
    row = at % rows
    dp = at // rows % dp_count
    x = at // (rows * dp_count) % x_count
    core = (at // (rows * dp_count * x_count) + lax.axis_index("core")) % 2
    column = ((dp * x_count + x) * 2 + core) * rows + row
    return (column[:, None] == at[None, :]).astype(LOW)


def add_low(a, b):
    return (a.astype(F32) + b.astype(F32)).astype(LOW)


def local(queries, out_grad, keys, values, neighbour_ids, neighbour_place, kv_weight):
    ring = ("pair", "side")
    owners = lax.axis_size("pair") * 2
    rows = kv_weight.shape[1]
    pair = [(i, i ^ 1) for i in range(owners)]
    near = [(i, (i + 1) % owners if i % 2 else (i - 1) % owners) for i in range(owners)]
    next_pair = [(i, (i + 2) % owners if i % 2 else (i - 2) % owners) for i in range(owners)]

    mine = jnp.transpose(kv_weight, (1, 0, 2)).reshape(rows, -1)
    along_dp = exchange(mine, ("dp", "side"))
    query_grad, kept, sent = attention(
        queries, out_grad, keys, values, neighbour_ids, neighbour_place, owners
    )
    received = lax.ppermute(sent, ring, pair)
    along_dp, kept = lax.optimization_barrier((along_dp, kept))
    same = exchange(along_dp, ("sx",))
    order = column_order(rows)
    same, order = lax.optimization_barrier((same, order))

    here = jnp.swapaxes(same, 2, 3).reshape(-1, 2 * mine.shape[1])
    weight = jnp.concatenate([here, lax.ppermute(here, "core", [(0, 1), (1, 0)])])

    left = lax.axis_index("side") == 0
    heads = [jnp.where(left, kept, received), jnp.where(left, received, kept)]
    raw = jnp.concatenate(heads, axis=2)
    raw = raw.reshape(owners // 2, -1, raw.shape[2])
    cap = kept.shape[0] * 2 // owners

    def project(chunk):
        return lax.optimization_barrier(dot_nt(chunk, weight).astype(LOW))

    opposite = lax.ppermute(project(raw[0]), ring, next_pair)
    other = lax.ppermute(project(raw[1]), ring, near)
    last = lax.ppermute(add_low(project(raw[2]), opposite), ring, next_pair)
    encoded = project(raw[3]).astype(F32) + other.astype(F32) + last.astype(F32)
    encoded = dot_nn(encoded.astype(LOW), order).astype(LOW)
    return (query_grad, encoded.reshape(cap, NBT, -1))


def solution(mesh):
    devices = mesh.devices
    dp_count, seq_count, enc_count = devices.shape
    split = Mesh(
        devices.reshape(dp_count, seq_count // 2, 2, enc_count // 2, 2),
        ("dp", "sx", "core", "pair", "side"),
    )
    group = ("dp", "sx", "core")
    ring = ("pair", "side")
    placed = (
        P(group, ring),
        P(group, ring),
        P(group, None, ring),
        P(group, None, ring),
        P(group, None),
        P(group, None),
        P(None, group, ring),
    )
    return jax.shard_map(
        local,
        mesh=split,
        in_specs=placed,
        out_specs=(P(group, ring), P(group + ring, None, None)),
        check_vma=False,
    )
```

time: 96.9 us -> 87.7 us (0.905)
  the two profiles are of different devices: /device:TPU:8 before, /device:TPU:40 now
where the time goes in v4:
time: 87.7 us; the launch traced here: 87.2 us
  waiting for transfers between devices  42.6 us (49%)
  starting transfers between devices  27.4 us (31%)
  Pallas kernels  5.9 us (7%)
  matrix products  4.46 us (5%)
  local copies, waits for them, and re-layouts  3.6 us (4%)
  other arithmetic  2.42 us (3%)
    all_to_all x2, starting transfers between devices, exchange(): lax.all_to_all(copies, axes, split_axis=0, concat_axis=0, tiled=True)  16.1 us
    all_to_all x2, waiting for transfers between devices, exchange(): lax.all_to_all(copies, axes, split_axis=0, concat_axis=0, tiled=True)  15.8 us
    ppermute x1, waiting for transfers between devices, local(): last = lax.ppermute(add_low(project(raw[2]), opposite), ring, next_pair)  11.5 us
    ppermute x1, waiting for transfers between devices, local(): opposite = lax.ppermute(project(raw[0]), ring, next_pair)  10.4 us
    pallas_call x1, Pallas kernels, attention(): pl.pallas_call(kernel, grid=(steps,), in_specs=[scalars, scalars, row_spe...  5.9 us
    ppermute x1, waiting for transfers between devices, local(): other = lax.ppermute(project(raw[1]), ring, near)  4.61 us
    dot_general x4, matrix products, dot_nt(): lax.dot_general(a, b, (((1,), (1,)), ((), ())), preferred_element_type=F32)  2.98 us
    ppermute x1, starting transfers between devices, local(): other = lax.ppermute(project(raw[1]), ring, near)  2.73 us
  transfers between devices with their start and end apart: 7, of which 7 were waited for; matrix products, arithmetic and copies ran while one was open for 8% of the time, Pallas kernels for 7%

profile of v4, /device:TPU:40, one launch (start us, length us, event | category | flops | bytes accessed | tf_op | source)
XLA Modules:
  0.0 87.2 jit_solution(10715899283355825908)
XLA Ops:
  0.6 0.7 pad.4
  1.4 0.7 broadcast_in_dim.7
  2.1 11.8 %all-to-all-start = ((bf16[16,14,512]{2,1,0:T(8,128)(2,1)}), bf16[16,14,512]{2,1,0:T(8,128)(2,1)S(1)}, u32[]{:S(2)}, u32[]{:S(2)}) async-start(bf16[16,14,512]{2,1,0:T(8,128)(2,1)} %broadcast_in_dim.7), calls=%async_computation | async-start | bytes 524288 | tf_op jit(solution)/shard_map/all_to_all | solution.py:138
  13.9 5.9 %attention_back.1 = (bf16[512,256]{1,0:T(8,128)(2,1)}, bf16[8,128,512]{2,1,0:T(8,128)(2,1)}, bf16[8,128,512]{2,1,0:T(8,128)(2,1)}) custom-call(s32[2,8]{1,0:T(2,128)} %bitcast.35, s32[1,16]{1,0:T(1,128)} %refs_1_.1, bf16[512,256]{1,0:T(8,128)(2,1)} %refs_2_.1, bf16[512,256]{1,0:T(8,128)(2,1)} %refs_3_.1, bf16[16,128,256]{2,1,0:T(8,128)(2,1)} %refs_4_.1, ...), custom_call_target="tpu_custom_call" | custom-call | flops 1000000000 | bytes 6000000 | tf_op jit(solution)/shard_map/attention_back/pallas_call | solution.py:119
  19.8 2.0 %collective-permute-start = (bf16[8,128,512]{2,1,0:T(8,128)(2,1)}, bf16[8,128,512]{2,1,0:T(8,128)(2,1)}, u32[]{:S(2)}, u32[]{:S(2)}) collective-permute-start(bf16[8,128,512]{2,1,0:T(8,128)(2,1)} %get-tuple-element.12), channel_id=1, source_target_pairs={{0,1},{1,0},{2,3},{3,2},{4,5},{5,4},{6,7},{7,6},{8,9},{9,8},{10,11... | collective-permute-start | bytes 3145736 | tf_op jit(solution)/shard_map/ppermute | solution.py:171
  21.8 2.5 %all-to-all-done = bf16[16,14,512]{2,1,0:T(8,128)(2,1)S(1)} async-done(((bf16[16,14,512]{2,1,0:T(8,128)(2,1)}), bf16[16,14,512]{2,1,0:T(8,128)(2,1)S(1)}, u32[]{:S(2)}, u32[]{:S(2)}) %all-to-all-start) | async-done | bytes 229408 | tf_op jit(solution)/shard_map/all_to_all | solution.py:138
  24.3 0.2 copy.12
  24.6 0.2 copy.11
  24.8 1.4 %broadcast_in_dim.8 = bf16[4,8,2,14,512]{4,2,3,1,0:T(2,128)(2,1)} broadcast(bf16[8,2,14,512]{3,1,2,0:T(2,128)(2,1)S(1)} %copy.11), dimensions={1,2,3,4} | broadcast | bytes 1146880 | tf_op jit(solution)/shard_map/broadcast_in_dim | solution.py:137
  26.2 4.3 %all-to-all-start.1 = ((bf16[4,8,2,14,512]{4,2,3,1,0:T(2,128)(2,1)}), bf16[4,8,2,14,512]{4,2,3,1,0:T(2,128)(2,1)S(1)}, u32[]{:S(2)}, u32[]{:S(2)}) async-start(bf16[4,8,2,14,512]{4,2,3,1,0:T(2,128)(2,1)} %broadcast_in_dim.8), calls=%async_computation.1 | async-start | bytes 1835008 | tf_op jit(solution)/shard_map/all_to_all | solution.py:138
  30.5 0.3 fusion
  30.8 13.2 %all-to-all-done.1 = bf16[4,8,2,14,512]{4,2,3,1,0:T(2,128)(2,1)S(1)} async-done(((bf16[4,8,2,14,512]{4,2,3,1,0:T(2,128)(2,1)}), bf16[4,8,2,14,512]{4,2,3,1,0:T(2,128)(2,1)S(1)}, u32[]{:S(2)}, u32[]{:S(2)}) %all-to-all-start.1) | async-done | bytes 917536 | tf_op jit(solution)/shard_map/all_to_all | solution.py:138
  44.1 0.2 copy.14
  44.3 1.9 %collective-permute-start.1 = (bf16[448,1024]{1,0:T(8,128)(2,1)S(1)}, bf16[448,1024]{1,0:T(8,128)(2,1)S(1)}, u32[]{:S(2)}, u32[]{:S(2)}) collective-permute-start(bf16[448,1024]{1,0:T(8,128)(2,1)S(1)} %bitcast.24), channel_id=1, source_target_pairs={{0,8},{8,0},{1,9},{9,1},{2,10},{10,2},{3,11},{11,3},{4,12},{12,4},... | collective-permute-start | bytes 2752520 | tf_op jit(solution)/shard_map/ppermute | solution.py:178
  46.2 0.1 collective-permute-done
  46.3 1.7 %broadcast_select_fusion.1 = (bf16[8,128,512]{2,1,0:T(8,128)(2,1)S(1)}, bf16[8,128,512]{2,1,0:T(8,128)(2,1)S(1)}) fusion(bf16[8,128,512]{2,1,0:T(8,128)(2,1)} %get-tuple-element.11, bf16[8,128,512]{2,1,0:T(8,128)(2,1)} %collective-permute-done, pred[]{:T(512)S(6)} %eq.21), kind=kLoop, calls=%fused_computation.14 | loop fusion | flops 1048576 | bytes 4194305 | tf_op jit(solution)/shard_map/jit(_where)/select_n | solution.py:181
  48.0 0.3 fusion.2
  48.3 0.1 constant_dynamic-update-slice_fusion.1
  48.4 0.3 collective-permute-done.1
  48.6 0.1 constant_dynamic-update-slice_fusion
  48.7 0.7 convolution_convert_fusion
  49.5 2.7 %collective-permute-start.3 = (bf16[256,896]{1,0:T(8,128)(2,1)S(1)}, bf16[256,896]{1,0:T(8,128)(2,1)S(1)}, u32[]{:S(2)}, u32[]{:S(2)}) collective-permute-start(bf16[256,896]{1,0:T(8,128)(2,1)S(1)} %convolution_convert_fusion), channel_id=1, source_target_pairs={{0,6},{1,3},{2,0},{3,5},{4,2},{5,7},{6,4},{7,1},{8,14},{9,11},{10,... | collective-permute-start | bytes 1376264 | tf_op jit(solution)/shard_map/ppermute | solution.py:189
  52.2 0.7 convolution_convert_fusion.2
  52.9 0.7 convolution_convert_fusion.1
  53.7 2.7 %collective-permute-start.2 = (bf16[256,896]{1,0:T(8,128)(2,1)S(1)}, bf16[256,896]{1,0:T(8,128)(2,1)S(1)}, u32[]{:S(2)}, u32[]{:S(2)}) collective-permute-start(bf16[256,896]{1,0:T(8,128)(2,1)S(1)} %convolution_convert_fusion.2), channel_id=1, source_target_pairs={{0,7},{1,2},{2,1},{3,4},{4,3},{5,6},{6,5},{7,0},{8,15},{9,10},{10,... | collective-permute-start | bytes 1376264 | tf_op jit(solution)/shard_map/ppermute | solution.py:190
  56.4 10.4 %collective-permute-done.3 = bf16[256,896]{1,0:T(8,128)(2,1)S(1)} collective-permute-done((bf16[256,896]{1,0:T(8,128)(2,1)S(1)}, bf16[256,896]{1,0:T(8,128)(2,1)S(1)}, u32[]{:S(2)}, u32[]{:S(2)}) %collective-permute-start.3) | collective-permute-done | bytes 458784 | tf_op jit(solution)/shard_map/ppermute | solution.py:189
  66.8 0.1 add_convert_fusion.1
  66.9 1.9 %collective-permute-start.4 = (bf16[256,896]{1,0:T(8,128)(2,1)S(1)}, bf16[256,896]{1,0:T(8,128)(2,1)S(1)}, u32[]{:S(2)}, u32[]{:S(2)}) collective-permute-start(bf16[256,896]{1,0:T(8,128)(2,1)S(1)} %add_convert_fusion.1), channel_id=1, source_target_pairs={{0,6},{1,3},{2,0},{3,5},{4,2},{5,7},{6,4},{7,1},{8,14},{9,11},{10,... | collective-permute-start | bytes 1376264 | tf_op jit(solution)/shard_map/ppermute | solution.py:191
  68.9 0.7 convolution_convert_fusion.3
  69.6 4.6 %collective-permute-done.2 = bf16[256,896]{1,0:T(8,128)(2,1)S(1)} collective-permute-done((bf16[256,896]{1,0:T(8,128)(2,1)S(1)}, bf16[256,896]{1,0:T(8,128)(2,1)S(1)}, u32[]{:S(2)}, u32[]{:S(2)}) %collective-permute-start.2) | collective-permute-done | bytes 458784 | tf_op jit(solution)/shard_map/ppermute | solution.py:190
  74.2 11.5 %collective-permute-done.4 = bf16[256,896]{1,0:T(8,128)(2,1)S(1)} collective-permute-done((bf16[256,896]{1,0:T(8,128)(2,1)S(1)}, bf16[256,896]{1,0:T(8,128)(2,1)S(1)}, u32[]{:S(2)}, u32[]{:S(2)}) %collective-permute-start.4) | collective-permute-done | bytes 458784 | tf_op jit(solution)/shard_map/ppermute | solution.py:191
  85.7 1.5 %convolution_convert_fusion.4 = bf16[256,896]{1,0:T(8,128)(2,1)} fusion(bf16[896,896]{1,0:T(8,128)(2,1)S(1)} %fusion, bf16[256,896]{1,0:T(8,128)(2,1)S(1)} %collective-permute-done.4, bf16[256,896]{1,0:T(8,128)(2,1)S(1)} %collective-permute-done.2, bf16[256,896]{1,0:T(8,128)(2,1)S(1)} %convolution_convert_fusion.3), kind=kOutput, calls=%fused_computation.12 | convolution fusion | flops 412647424 | bytes 3440640 | tf_op jit(solution)/shard_map/dot_general | solution.py:30
  (2 shorter events, 0.0 us)
Async XLA Ops:
  2.1 22.2 %all-to-all-start = ((bf16[16,14,512]{2,1,0:T(8,128)(2,1)}), bf16[16,14,512]{2,1,0:T(8,128)(2,1)S(1)}, u32[]{:S(2)}, u32[]{:S(2)}) async-start(bf16[16,14,512]{2,1,0:T(8,128)(2,1)} %broadcast_in_dim.7), calls=%async_computation | async-start | bytes 524288 | tf_op jit(solution)/shard_map/all_to_all | solution.py:138
  19.8 26.6 %collective-permute-start = (bf16[8,128,512]{2,1,0:T(8,128)(2,1)}, bf16[8,128,512]{2,1,0:T(8,128)(2,1)}, u32[]{:S(2)}, u32[]{:S(2)}) collective-permute-start(bf16[8,128,512]{2,1,0:T(8,128)(2,1)} %get-tuple-element.12), channel_id=1, source_target_pairs={{0,1},{1,0},{2,3},{3,2},{4,5},{5,4},{6,7},{7,6},{8,9},{9,8},{10,11... | collective-permute-start | bytes 3145736 | tf_op jit(solution)/shard_map/ppermute | solution.py:171
  26.2 17.9 %all-to-all-start.1 = ((bf16[4,8,2,14,512]{4,2,3,1,0:T(2,128)(2,1)}), bf16[4,8,2,14,512]{4,2,3,1,0:T(2,128)(2,1)S(1)}, u32[]{:S(2)}, u32[]{:S(2)}) async-start(bf16[4,8,2,14,512]{4,2,3,1,0:T(2,128)(2,1)} %broadcast_in_dim.8), calls=%async_computation.1 | async-start | bytes 1835008 | tf_op jit(solution)/shard_map/all_to_all | solution.py:138
  44.3 4.4 %collective-permute-start.1 = (bf16[448,1024]{1,0:T(8,128)(2,1)S(1)}, bf16[448,1024]{1,0:T(8,128)(2,1)S(1)}, u32[]{:S(2)}, u32[]{:S(2)}) collective-permute-start(bf16[448,1024]{1,0:T(8,128)(2,1)S(1)} %bitcast.24), channel_id=1, source_target_pairs={{0,8},{8,0},{1,9},{9,1},{2,10},{10,2},{3,11},{11,3},{4,12},{12,4},... | collective-permute-start | bytes 2752520 | tf_op jit(solution)/shard_map/ppermute | solution.py:178
  49.5 17.4 %collective-permute-start.3 = (bf16[256,896]{1,0:T(8,128)(2,1)S(1)}, bf16[256,896]{1,0:T(8,128)(2,1)S(1)}, u32[]{:S(2)}, u32[]{:S(2)}) collective-permute-start(bf16[256,896]{1,0:T(8,128)(2,1)S(1)} %convolution_convert_fusion), channel_id=1, source_target_pairs={{0,6},{1,3},{2,0},{3,5},{4,2},{5,7},{6,4},{7,1},{8,14},{9,11},{10,... | collective-permute-start | bytes 1376264 | tf_op jit(solution)/shard_map/ppermute | solution.py:189
  53.7 20.6 %collective-permute-start.2 = (bf16[256,896]{1,0:T(8,128)(2,1)S(1)}, bf16[256,896]{1,0:T(8,128)(2,1)S(1)}, u32[]{:S(2)}, u32[]{:S(2)}) collective-permute-start(bf16[256,896]{1,0:T(8,128)(2,1)S(1)} %convolution_convert_fusion.2), channel_id=1, source_target_pairs={{0,7},{1,2},{2,1},{3,4},{4,3},{5,6},{6,5},{7,0},{8,15},{9,10},{10,... | collective-permute-start | bytes 1376264 | tf_op jit(solution)/shard_map/ppermute | solution.py:190
  66.9 18.7 %collective-permute-start.4 = (bf16[256,896]{1,0:T(8,128)(2,1)S(1)}, bf16[256,896]{1,0:T(8,128)(2,1)S(1)}, u32[]{:S(2)}, u32[]{:S(2)}) collective-permute-start(bf16[256,896]{1,0:T(8,128)(2,1)S(1)} %add_convert_fusion.1), channel_id=1, source_target_pairs={{0,6},{1,3},{2,0},{3,5},{4,2},{5,7},{6,4},{7,1},{8,14},{9,11},{10,... | collective-permute-start | bytes 1376264 | tf_op jit(solution)/shard_map/ppermute | solution.py:191

commit v5 on v4

--- a/solution.py
+++ b/solution.py
@@ -12,7 +12,7 @@
 SPAN = 64
 NBT = 128
 NEIGH = 2
-STEP_SPANS = 4
+STEP_SPANS = 8
 
 LOW = jnp.bfloat16
 F32 = jnp.float32
@@ -52,19 +52,16 @@
 
 def attention_kernel(heads, owners, ids, place, q_ref, g_ref, k_ref, v_ref, dq_ref, kept_ref, *rest):
     *sent_refs, total = rest
-    step = pl.program_id(0)
     factor = 1.0 / math.sqrt(HD)
     width = heads * HD
     me = lax.axis_index("pair") * 2 + lax.axis_index("side")
 
-    @pl.when(step == 0)
-    def _():
-        total[...] = jnp.zeros_like(total)
+    total[...] = jnp.zeros_like(total)
 
     slots = []
     for s in range(STEP_SPANS):
         for j in range(NEIGH):
-            entry = place[0, ids[j, step * STEP_SPANS + s]]
+            entry = place[0, ids[j, s]]
             slots.append(entry_place(me, entry, owners))
 
     def rows_of(ref, unit):
@@ -92,26 +89,25 @@
             total[slot, :, h * HD : (h + 1) * HD] += key_grad[part]
             total[slot, :, width + h * HD : width + (h + 1) * HD] += value_grad[part]
 
-    @pl.when(step == pl.num_programs(0) - 1)
-    def _():
-        first = 0
-        for ref in (kept_ref, *sent_refs):
-            part = slice(first, first + ref.shape[0])
-            ref[:, :, :width] = (total[part, :, :width] * factor).astype(LOW)
-            ref[:, :, width:] = total[part, :, width:].astype(LOW)
-            first += ref.shape[0]
+    first = 0
+    for ref in (kept_ref, *sent_refs):
+        part = slice(first, first + ref.shape[0])
+        ref[:, :, :width] = (total[part, :, :width] * factor).astype(LOW)
+        ref[:, :, width:] = total[part, :, width:].astype(LOW)
+        first += ref.shape[0]
 
 
 def attention(queries, out_grad, keys, values, ids, place, owners):
     tokens, width = queries.shape
     slots = keys.shape[0]
     entries = place.shape[1]
+    cap = entries // owners
     steps = slots // (NEIGH * STEP_SPANS)
     row_spec = pl.BlockSpec((STEP_SPANS * SPAN, width), lambda i: (i, 0))
     slot_spec = pl.BlockSpec((STEP_SPANS * NEIGH, NBT, width), lambda i: (i, 0, 0))
     scalars = pl.BlockSpec(memory_space=pltpu.SMEM)
 
-    shapes = [(entries // 2, NBT, 2 * width)] * 2
+    shapes = [(n, NBT, 2 * width) for n in (entries // 2, entries // 2 - cap, cap)]
 
     def kernel(*refs):
         attention_kernel(width // HD, owners, *refs)
@@ -165,31 +161,38 @@
 
     mine = jnp.transpose(kv_weight, (1, 0, 2)).reshape(rows, -1)
     along_dp = exchange(mine, ("dp", "side"))
-    query_grad, kept, sent = attention(
+    query_grad, kept, sent, sent_own = attention(
         queries, out_grad, keys, values, neighbour_ids, neighbour_place, owners
     )
     received = lax.ppermute(sent, ring, pair)
     along_dp, kept = lax.optimization_barrier((along_dp, kept))
     same = exchange(along_dp, ("sx",))
     order = column_order(rows)
-    same, order = lax.optimization_barrier((same, order))
+    same, order, received = lax.optimization_barrier((same, order, received))
 
     here = jnp.swapaxes(same, 2, 3).reshape(-1, 2 * mine.shape[1])
     weight = jnp.concatenate([here, lax.ppermute(here, "core", [(0, 1), (1, 0)])])
 
     left = lax.axis_index("side") == 0
-    heads = [jnp.where(left, kept, received), jnp.where(left, received, kept)]
-    raw = jnp.concatenate(heads, axis=2)
-    raw = raw.reshape(owners // 2, -1, raw.shape[2])
-    cap = kept.shape[0] * 2 // owners
+    cap = sent_own.shape[0]
+
+    def both_heads(mine, theirs):
+        heads = [jnp.where(left, mine, theirs), jnp.where(left, theirs, mine)]
+        raw = jnp.concatenate(heads, axis=2)
+        return raw.reshape(-1, cap * NBT, raw.shape[2])
+
+    raw = both_heads(kept[:-cap], received)
 
     def project(chunk):
         return lax.optimization_barrier(dot_nt(chunk, weight).astype(LOW))
 
-    opposite = lax.ppermute(project(raw[0]), ring, next_pair)
+    part = project(raw[0])
+    opposite = lax.ppermute(part, ring, next_pair)
     other = lax.ppermute(project(raw[1]), ring, near)
+    sent_own, _ = lax.optimization_barrier((sent_own, part))
+    own = both_heads(kept[-cap:], lax.ppermute(sent_own, ring, pair))[0]
     last = lax.ppermute(add_low(project(raw[2]), opposite), ring, next_pair)
-    encoded = project(raw[3]).astype(F32) + other.astype(F32) + last.astype(F32)
+    encoded = project(own).astype(F32) + other.astype(F32) + last.astype(F32)
     encoded = dot_nn(encoded.astype(LOW), order).astype(LOW)
     return (query_grad, encoded.reshape(cap, NBT, -1))
 

time: 87.7 us -> 87.8 us (level)
  the two profiles are of different devices: /device:TPU:40 before, /device:TPU:8 now
where the time goes in v5:
time: 87.8 us; the launch traced here: 87.2 us
  waiting for transfers between devices  35.5 us (40%)
  starting transfers between devices  35.1 us (40%)
  Pallas kernels  5.54 us (6%)
  local copies, waits for them, and re-layouts  5 us (6%)
  matrix products  4.46 us (5%)
    all_to_all x2, starting transfers between devices, exchange(): lax.all_to_all(copies, axes, split_axis=0, concat_axis=0, tiled=True)  16.1 us
    ppermute x1, waiting for transfers between devices, local(): last = lax.ppermute(add_low(project(raw[2]), opposite), ring, next_pair)  11 us
    ppermute x1, waiting for transfers between devices, local(): received = lax.ppermute(sent, ring, pair)  9.39 us
    all_to_all x2, waiting for transfers between devices, exchange(): lax.all_to_all(copies, axes, split_axis=0, concat_axis=0, tiled=True)  6.75 us
    pallas_call x1, Pallas kernels, attention(): pl.pallas_call(kernel, grid=(steps,), in_specs=[scalars, scalars, row_spe...  5.54 us
    ppermute x1, starting transfers between devices, local(): other = lax.ppermute(project(raw[1]), ring, near)  5.36 us
    ppermute x1, starting transfers between devices, local(): opposite = lax.ppermute(part, ring, next_pair)  4.5 us
    ppermute x1, waiting for transfers between devices, local(): opposite = lax.ppermute(part, ring, next_pair)  4.09 us
  transfers between devices with their start and end apart: 8, of which 8 were waited for; matrix products, arithmetic and copies ran while one was open for 6% of the time, Pallas kernels for 6%

profile of v5, /device:TPU:8, one launch (start us, length us, event | category | flops | bytes accessed | tf_op | source)
XLA Modules:
  0.0 87.2 jit_solution(937225347682729218)
XLA Ops:
  0.6 0.7 pad.6
  1.4 0.7 broadcast_in_dim.7
  2.1 11.8 %all-to-all-start = ((bf16[16,14,512]{2,1,0:T(8,128)(2,1)}), bf16[16,14,512]{2,1,0:T(8,128)(2,1)S(1)}, u32[]{:S(2)}, u32[]{:S(2)}) async-start(bf16[16,14,512]{2,1,0:T(8,128)(2,1)} %broadcast_in_dim.7), calls=%async_computation | async-start | bytes 524288 | tf_op jit(solution)/shard_map/all_to_all | solution.py:134
  13.9 5.5 %attention_back.1 = (bf16[512,256]{1,0:T(8,128)(2,1)}, bf16[8,128,512]{2,1,0:T(8,128)(2,1)}, bf16[6,128,512]{2,1,0:T(8,128)(2,1)}, bf16[2,128,512]{2,1,0:T(8,128)(2,1)}) custom-call(s32[2,8]{1,0:T(2,128)} %bitcast.35, s32[1,16]{1,0:T(1,128)} %refs_1_.1, bf16[512,256]{1,0:T(8,128)(2,1)} %refs_2_.1, bf16[512,256]{1,0:T(8,128)(2,1)} %refs_3_.1, ...), custom_call_target="tpu_custom_call" | custom-call | flops 1000000000 | bytes 6000000 | tf_op jit(solution)/shard_map/attention_back/pallas_call | solution.py:115
  19.4 2.0 %collective-permute-start = (bf16[6,128,512]{2,1,0:T(8,128)(2,1)}, bf16[6,128,512]{2,1,0:T(8,128)(2,1)S(1)}, u32[]{:S(2)}, u32[]{:S(2)}) collective-permute-start(bf16[6,128,512]{2,1,0:T(8,128)(2,1)} %get-tuple-element.17), channel_id=1, source_target_pairs={{0,1},{1,0},{2,3},{3,2},{4,5},{5,4},{6,7},{7,6},{8,9},{9,8},{10,11... | collective-permute-start | bytes 2359304 | tf_op jit(solution)/shard_map/ppermute | solution.py:167
  21.5 2.9 %all-to-all-done = bf16[16,14,512]{2,1,0:T(8,128)(2,1)S(1)} async-done(((bf16[16,14,512]{2,1,0:T(8,128)(2,1)}), bf16[16,14,512]{2,1,0:T(8,128)(2,1)S(1)}, u32[]{:S(2)}, u32[]{:S(2)}) %all-to-all-start) | async-done | bytes 229408 | tf_op jit(solution)/shard_map/all_to_all | solution.py:134
  24.4 0.2 copy.12
  24.6 0.2 copy.11
  24.8 1.4 %broadcast_in_dim.8 = bf16[4,8,2,14,512]{4,2,3,1,0:T(2,128)(2,1)} broadcast(bf16[8,2,14,512]{3,1,2,0:T(2,128)(2,1)S(1)} %copy.11), dimensions={1,2,3,4} | broadcast | bytes 1146880 | tf_op jit(solution)/shard_map/broadcast_in_dim | solution.py:133
  26.2 4.3 %all-to-all-start.1 = ((bf16[4,8,2,14,512]{4,2,3,1,0:T(2,128)(2,1)}), bf16[4,8,2,14,512]{4,2,3,1,0:T(2,128)(2,1)S(1)}, u32[]{:S(2)}, u32[]{:S(2)}) async-start(bf16[4,8,2,14,512]{4,2,3,1,0:T(2,128)(2,1)} %broadcast_in_dim.8), calls=%async_computation.1 | async-start | bytes 1835008 | tf_op jit(solution)/shard_map/all_to_all | solution.py:134
  30.5 0.3 fusion
  30.9 9.4 %collective-permute-done = bf16[6,128,512]{2,1,0:T(8,128)(2,1)S(1)} collective-permute-done((bf16[6,128,512]{2,1,0:T(8,128)(2,1)}, bf16[6,128,512]{2,1,0:T(8,128)(2,1)S(1)}, u32[]{:S(2)}, u32[]{:S(2)}) %collective-permute-start) | collective-permute-done | bytes 786464 | tf_op jit(solution)/shard_map/ppermute | solution.py:167
  40.3 3.8 %all-to-all-done.1 = bf16[4,8,2,14,512]{4,2,3,1,0:T(2,128)(2,1)S(1)} async-done(((bf16[4,8,2,14,512]{4,2,3,1,0:T(2,128)(2,1)}), bf16[4,8,2,14,512]{4,2,3,1,0:T(2,128)(2,1)S(1)}, u32[]{:S(2)}, u32[]{:S(2)}) %all-to-all-start.1) | async-done | bytes 917536 | tf_op jit(solution)/shard_map/all_to_all | solution.py:134
  44.1 0.2 copy.14
  44.3 1.9 %collective-permute-start.1 = (bf16[448,1024]{1,0:T(8,128)(2,1)S(1)}, bf16[448,1024]{1,0:T(8,128)(2,1)S(1)}, u32[]{:S(2)}, u32[]{:S(2)}) collective-permute-start(bf16[448,1024]{1,0:T(8,128)(2,1)S(1)} %bitcast.25), channel_id=1, source_target_pairs={{0,8},{8,0},{1,9},{9,1},{2,10},{10,2},{3,11},{11,3},{4,12},{12,4},... | collective-permute-start | bytes 2752520 | tf_op jit(solution)/shard_map/ppermute | solution.py:174
  46.3 1.1 %copy-done = bf16[8,128,512]{2,1,0:T(8,128)(2,1)S(1)} copy-done((bf16[8,128,512]{2,1,0:T(8,128)(2,1)S(1)}, bf16[8,128,512]{2,1,0:T(8,128)(2,1)}, u32[]{:S(2)}) %copy-start) | copy-done | bytes 1048600
  47.5 0.2 copy-done.2
  47.8 0.2 fusion.1
  48.0 0.7 collective-permute-done.1
  48.7 0.7 convolution_convert_fusion.3
  49.5 4.5 %collective-permute-start.4 = (bf16[256,896]{1,0:T(8,128)(2,1)S(1)}, bf16[256,896]{1,0:T(8,128)(2,1)S(1)}, u32[]{:S(2)}, u32[]{:S(2)}) collective-permute-start(bf16[256,896]{1,0:T(8,128)(2,1)S(1)} %convolution_convert_fusion.3), channel_id=1, source_target_pairs={{0,6},{1,3},{2,0},{3,5},{4,2},{5,7},{6,4},{7,1},{8,14},{9,11},{10,... | collective-permute-start | bytes 1376264 | tf_op jit(solution)/shard_map/ppermute | solution.py:190
  54.0 1.9 %collective-permute-start.2 = (bf16[2,128,512]{2,1,0:T(8,128)(2,1)S(1)}, bf16[2,128,512]{2,1,0:T(8,128)(2,1)S(1)}, u32[]{:S(2)}, u32[]{:S(2)}) collective-permute-start(bf16[2,128,512]{2,1,0:T(8,128)(2,1)S(1)} %copy-done.3), channel_id=1, source_target_pairs={{0,1},{1,0},{2,3},{3,2},{4,5},{5,4},{6,7},{7,6},{8,9},{9,8},{10,11... | collective-permute-start | bytes 786440 | tf_op jit(solution)/shard_map/ppermute | solution.py:193
  55.9 0.7 convolution_convert_fusion
  56.7 0.7 convolution_convert_fusion.1
  57.5 5.4 %collective-permute-start.3 = (bf16[256,896]{1,0:T(8,128)(2,1)S(1)}, bf16[256,896]{1,0:T(8,128)(2,1)S(1)}, u32[]{:S(2)}, u32[]{:S(2)}) collective-permute-start(bf16[256,896]{1,0:T(8,128)(2,1)S(1)} %convolution_convert_fusion.1), channel_id=1, source_target_pairs={{0,7},{1,2},{2,1},{3,4},{4,3},{5,6},{6,5},{7,0},{8,15},{9,10},{10,... | collective-permute-start | bytes 1376264 | tf_op jit(solution)/shard_map/ppermute | solution.py:191
  62.8 4.1 %collective-permute-done.4 = bf16[256,896]{1,0:T(8,128)(2,1)S(1)} collective-permute-done((bf16[256,896]{1,0:T(8,128)(2,1)S(1)}, bf16[256,896]{1,0:T(8,128)(2,1)S(1)}, u32[]{:S(2)}, u32[]{:S(2)}) %collective-permute-start.4) | collective-permute-done | bytes 458784 | tf_op jit(solution)/shard_map/ppermute | solution.py:190
  67.0 3.3 %collective-permute-start.5 = (bf16[256,896]{1,0:T(8,128)(2,1)S(1)}, bf16[256,896]{1,0:T(8,128)(2,1)S(1)}, u32[]{:S(2)}, u32[]{:S(2)}) collective-permute-start(bf16[256,896]{1,0:T(8,128)(2,1)S(1)} %add_convert_fusion.1), channel_id=1, source_target_pairs={{0,6},{1,3},{2,0},{3,5},{4,2},{5,7},{6,4},{7,1},{8,14},{9,11},{10,... | collective-permute-start | bytes 1376264 | tf_op jit(solution)/shard_map/ppermute | solution.py:194
  70.3 1.4 %collective-permute-done.2 = bf16[2,128,512]{2,1,0:T(8,128)(2,1)S(1)} collective-permute-done((bf16[2,128,512]{2,1,0:T(8,128)(2,1)S(1)}, bf16[2,128,512]{2,1,0:T(8,128)(2,1)S(1)}, u32[]{:S(2)}, u32[]{:S(2)}) %collective-permute-start.2) | collective-permute-done | bytes 262176 | tf_op jit(solution)/shard_map/ppermute | solution.py:193
  71.8 0.7 convolution_convert_fusion.2
  72.5 2.2 %collective-permute-done.3 = bf16[256,896]{1,0:T(8,128)(2,1)S(1)} collective-permute-done((bf16[256,896]{1,0:T(8,128)(2,1)S(1)}, bf16[256,896]{1,0:T(8,128)(2,1)S(1)}, u32[]{:S(2)}, u32[]{:S(2)}) %collective-permute-start.3) | collective-permute-done | bytes 458784 | tf_op jit(solution)/shard_map/ppermute | solution.py:191
  74.7 11.0 %collective-permute-done.5 = bf16[256,896]{1,0:T(8,128)(2,1)S(1)} collective-permute-done((bf16[256,896]{1,0:T(8,128)(2,1)S(1)}, bf16[256,896]{1,0:T(8,128)(2,1)S(1)}, u32[]{:S(2)}, u32[]{:S(2)}) %collective-permute-start.5) | collective-permute-done | bytes 458784 | tf_op jit(solution)/shard_map/ppermute | solution.py:194
  85.8 1.5 %convolution_convert_fusion.4 = bf16[256,896]{1,0:T(8,128)(2,1)} fusion(bf16[896,896]{1,0:T(8,128)(2,1)S(1)} %fusion, bf16[256,896]{1,0:T(8,128)(2,1)S(1)} %collective-permute-done.5, bf16[256,896]{1,0:T(8,128)(2,1)S(1)} %collective-permute-done.3, bf16[256,896]{1,0:T(8,128)(2,1)S(1)} %convolution_convert_fusion.2), kind=kOutput, calls=%fused_computation.10 | convolution fusion | flops 412647424 | bytes 3440640 | tf_op jit(solution)/shard_map/dot_general | solution.py:30
  (14 shorter events, 0.5 us)
Async XLA Ops:
  2.1 22.2 %all-to-all-start = ((bf16[16,14,512]{2,1,0:T(8,128)(2,1)}), bf16[16,14,512]{2,1,0:T(8,128)(2,1)S(1)}, u32[]{:S(2)}, u32[]{:S(2)}) async-start(bf16[16,14,512]{2,1,0:T(8,128)(2,1)} %broadcast_in_dim.7), calls=%async_computation | async-start | bytes 524288 | tf_op jit(solution)/shard_map/all_to_all | solution.py:134
  19.4 20.8 %collective-permute-start = (bf16[6,128,512]{2,1,0:T(8,128)(2,1)}, bf16[6,128,512]{2,1,0:T(8,128)(2,1)S(1)}, u32[]{:S(2)}, u32[]{:S(2)}) collective-permute-start(bf16[6,128,512]{2,1,0:T(8,128)(2,1)} %get-tuple-element.17), channel_id=1, source_target_pairs={{0,1},{1,0},{2,3},{3,2},{4,5},{5,4},{6,7},{7,6},{8,9},{9,8},{10,11... | collective-permute-start | bytes 2359304 | tf_op jit(solution)/shard_map/ppermute | solution.py:167
  26.2 17.9 %all-to-all-start.1 = ((bf16[4,8,2,14,512]{4,2,3,1,0:T(2,128)(2,1)}), bf16[4,8,2,14,512]{4,2,3,1,0:T(2,128)(2,1)S(1)}, u32[]{:S(2)}, u32[]{:S(2)}) async-start(bf16[4,8,2,14,512]{4,2,3,1,0:T(2,128)(2,1)} %broadcast_in_dim.8), calls=%async_computation.1 | async-start | bytes 1835008 | tf_op jit(solution)/shard_map/all_to_all | solution.py:134
  40.3 3.8 %copy-start.1 = (bf16[6,128,512]{2,1,0:T(8,128)(2,1)}, bf16[6,128,512]{2,1,0:T(8,128)(2,1)S(1)}, u32[]{:S(2)}) copy-start(bf16[6,128,512]{2,1,0:T(8,128)(2,1)S(1)} %collective-permute-done) | copy-start | bytes 2359300
  44.3 4.4 %collective-permute-start.1 = (bf16[448,1024]{1,0:T(8,128)(2,1)S(1)}, bf16[448,1024]{1,0:T(8,128)(2,1)S(1)}, u32[]{:S(2)}, u32[]{:S(2)}) collective-permute-start(bf16[448,1024]{1,0:T(8,128)(2,1)S(1)} %bitcast.25), channel_id=1, source_target_pairs={{0,8},{8,0},{1,9},{9,1},{2,10},{10,2},{3,11},{11,3},{4,12},{12,4},... | collective-permute-start | bytes 2752520 | tf_op jit(solution)/shard_map/ppermute | solution.py:174
  46.2 1.2 %copy-start = (bf16[8,128,512]{2,1,0:T(8,128)(2,1)S(1)}, bf16[8,128,512]{2,1,0:T(8,128)(2,1)}, u32[]{:S(2)}) copy-start(bf16[8,128,512]{2,1,0:T(8,128)(2,1)} %get-tuple-element.14) | copy-start | bytes 3145732
  46.2 1.4 %copy-start.2 = (bf16[6,128,512]{2,1,0:T(8,128)(2,1)S(1)}, bf16[6,128,512]{2,1,0:T(8,128)(2,1)}, u32[]{:S(2)}) copy-start(bf16[6,128,512]{2,1,0:T(8,128)(2,1)} %copy-done.1) | copy-start | bytes 2359300
  48.7 5.3 %copy-start.3 = (bf16[2,128,512]{2,1,0:T(8,128)(2,1)S(1)}, bf16[2,128,512]{2,1,0:T(8,128)(2,1)}, u32[]{:S(2)}) copy-start(bf16[2,128,512]{2,1,0:T(8,128)(2,1)} %get-tuple-element.20) | copy-start | bytes 786436
  49.5 17.4 %collective-permute-start.4 = (bf16[256,896]{1,0:T(8,128)(2,1)S(1)}, bf16[256,896]{1,0:T(8,128)(2,1)S(1)}, u32[]{:S(2)}, u32[]{:S(2)}) collective-permute-start(bf16[256,896]{1,0:T(8,128)(2,1)S(1)} %convolution_convert_fusion.3), channel_id=1, source_target_pairs={{0,6},{1,3},{2,0},{3,5},{4,2},{5,7},{6,4},{7,1},{8,14},{9,11},{10,... | collective-permute-start | bytes 1376264 | tf_op jit(solution)/shard_map/ppermute | solution.py:190
  54.0 17.7 %collective-permute-start.2 = (bf16[2,128,512]{2,1,0:T(8,128)(2,1)S(1)}, bf16[2,128,512]{2,1,0:T(8,128)(2,1)S(1)}, u32[]{:S(2)}, u32[]{:S(2)}) collective-permute-start(bf16[2,128,512]{2,1,0:T(8,128)(2,1)S(1)} %copy-done.3), channel_id=1, source_target_pairs={{0,1},{1,0},{2,3},{3,2},{4,5},{5,4},{6,7},{7,6},{8,9},{9,8},{10,11... | collective-permute-start | bytes 786440 | tf_op jit(solution)/shard_map/ppermute | solution.py:193
  57.5 17.3 %collective-permute-start.3 = (bf16[256,896]{1,0:T(8,128)(2,1)S(1)}, bf16[256,896]{1,0:T(8,128)(2,1)S(1)}, u32[]{:S(2)}, u32[]{:S(2)}) collective-permute-start(bf16[256,896]{1,0:T(8,128)(2,1)S(1)} %convolution_convert_fusion.1), channel_id=1, source_target_pairs={{0,7},{1,2},{2,1},{3,4},{4,3},{5,6},{6,5},{7,0},{8,15},{9,10},{10,... | collective-permute-start | bytes 1376264 | tf_op jit(solution)/shard_map/ppermute | solution.py:191
  67.0 18.7 %collective-permute-start.5 = (bf16[256,896]{1,0:T(8,128)(2,1)S(1)}, bf16[256,896]{1,0:T(8,128)(2,1)S(1)}, u32[]{:S(2)}, u32[]{:S(2)}) collective-permute-start(bf16[256,896]{1,0:T(8,128)(2,1)S(1)} %add_convert_fusion.1), channel_id=1, source_target_pairs={{0,6},{1,3},{2,0},{3,5},{4,2},{5,7},{6,4},{7,1},{8,14},{9,11},{10,... | collective-permute-start | bytes 1376264 | tf_op jit(solution)/shard_map/ppermute | solution.py:194

commit v6 on v4

--- a/solution.py
+++ b/solution.py
@@ -163,8 +163,7 @@
     near = [(i, (i + 1) % owners if i % 2 else (i - 1) % owners) for i in range(owners)]
     next_pair = [(i, (i + 2) % owners if i % 2 else (i - 2) % owners) for i in range(owners)]
 
-    mine = jnp.transpose(kv_weight, (1, 0, 2)).reshape(rows, -1)
-    along_dp = exchange(mine, ("dp", "side"))
+    along_dp = exchange(kv_weight, ("dp", "side"))
     query_grad, kept, sent = attention(
         queries, out_grad, keys, values, neighbour_ids, neighbour_place, owners
     )
@@ -174,7 +173,7 @@
     order = column_order(rows)
     same, order = lax.optimization_barrier((same, order))
 
-    here = jnp.swapaxes(same, 2, 3).reshape(-1, 2 * mine.shape[1])
+    here = jnp.transpose(same, (0, 1, 4, 2, 3, 5)).reshape(-1, 4 * kv_weight.shape[2])
     weight = jnp.concatenate([here, lax.ppermute(here, "core", [(0, 1), (1, 0)])])
 
     left = lax.axis_index("side") == 0

time: 87.7 us -> 87.4 us (level)
  the two profiles are of different devices: /device:TPU:40 before, /device:TPU:8 now
where the time goes in v6:
time: 87.4 us; the launch traced here: 86.9 us
  waiting for transfers between devices  39.7 us (45%)
  starting transfers between devices  29.7 us (34%)
  Pallas kernels  5.9 us (7%)
  matrix products  4.46 us (5%)
  local copies, waits for them, and re-layouts  3.89 us (4%)
  other arithmetic  2.42 us (3%)
    all_to_all x2, starting transfers between devices, exchange(): lax.all_to_all(copies, axes, split_axis=0, concat_axis=0, tiled=True)  16.1 us
    all_to_all x2, waiting for transfers between devices, exchange(): lax.all_to_all(copies, axes, split_axis=0, concat_axis=0, tiled=True)  15.2 us
    ppermute x1, waiting for transfers between devices, local(): last = lax.ppermute(add_low(project(raw[2]), opposite), ring, next_pair)  10.9 us
    ppermute x1, waiting for transfers between devices, local(): opposite = lax.ppermute(project(raw[0]), ring, next_pair)  9.45 us
    pallas_call x1, Pallas kernels, attention(): pl.pallas_call(kernel, grid=(steps,), in_specs=[scalars, scalars, row_spe...  5.9 us
    ppermute x1, starting transfers between devices, local(): opposite = lax.ppermute(project(raw[0]), ring, next_pair)  4.49 us
    ppermute x1, waiting for transfers between devices, local(): other = lax.ppermute(project(raw[1]), ring, near)  3.67 us
    ppermute x1, starting transfers between devices, local(): last = lax.ppermute(add_low(project(raw[2]), opposite), ring, next_pair)  3.28 us
  transfers between devices with their start and end apart: 7, of which 6 were waited for; matrix products, arithmetic and copies ran while one was open for 8% of the time, Pallas kernels for 7%

profile of v6, /device:TPU:8, one launch (start us, length us, event | category | flops | bytes accessed | tf_op | source)
XLA Modules:
  0.0 86.9 jit_solution(1996864771243762400)
XLA Ops:
  0.6 1.5 %broadcast_in_dim.4 = bf16[16,2,14,256]{3,1,2,0:T(2,128)(2,1)} broadcast(bf16[2,14,256]{2,0,1:T(2,128)(2,1)} %param.13), dimensions={1,2,3} | broadcast | bytes 243712 | tf_op jit(solution)/shard_map/broadcast_in_dim | solution.py:137
  2.1 11.8 %all-to-all-start = ((bf16[16,2,14,256]{3,1,2,0:T(2,128)(2,1)}), bf16[16,2,14,256]{3,1,2,0:T(2,128)(2,1)S(1)}, u32[]{:S(2)}, u32[]{:S(2)}) async-start(bf16[16,2,14,256]{3,1,2,0:T(2,128)(2,1)} %broadcast_in_dim.4), calls=%async_computation | async-start | bytes 458752 | tf_op jit(solution)/shard_map/all_to_all | solution.py:138
  13.9 5.9 %attention_back.1 = (bf16[512,256]{1,0:T(8,128)(2,1)}, bf16[8,128,512]{2,1,0:T(8,128)(2,1)}, bf16[8,128,512]{2,1,0:T(8,128)(2,1)}) custom-call(s32[2,8]{1,0:T(2,128)} %bitcast.23, s32[1,16]{1,0:T(1,128)} %refs_1_.1, bf16[512,256]{1,0:T(8,128)(2,1)} %refs_2_.1, bf16[512,256]{1,0:T(8,128)(2,1)} %refs_3_.1, bf16[16,128,256]{2,1,0:T(8,128)(2,1)} %refs_4_.1, ...), custom_call_target="tpu_custom_call" | custom-call | flops 1000000000 | bytes 6000000 | tf_op jit(solution)/shard_map/attention_back/pallas_call | solution.py:119
  19.8 2.0 %collective-permute-start = (bf16[8,128,512]{2,1,0:T(8,128)(2,1)}, bf16[8,128,512]{2,1,0:T(8,128)(2,1)}, u32[]{:S(2)}, u32[]{:S(2)}) collective-permute-start(bf16[8,128,512]{2,1,0:T(8,128)(2,1)} %get-tuple-element.12), channel_id=1, source_target_pairs={{0,1},{1,0},{2,3},{3,2},{4,5},{5,4},{6,7},{7,6},{8,9},{9,8},{10,11... | collective-permute-start | bytes 3145736 | tf_op jit(solution)/shard_map/ppermute | solution.py:170
  21.9 2.3 %all-to-all-done = bf16[16,2,14,256]{3,1,2,0:T(2,128)(2,1)S(1)} async-done(((bf16[16,2,14,256]{3,1,2,0:T(2,128)(2,1)}), bf16[16,2,14,256]{3,1,2,0:T(2,128)(2,1)S(1)}, u32[]{:S(2)}, u32[]{:S(2)}) %all-to-all-start) | async-done | bytes 229408 | tf_op jit(solution)/shard_map/all_to_all | solution.py:138
  24.2 0.2 copy.11
  24.4 1.4 %broadcast_in_dim.5 = bf16[4,8,2,2,14,256]{5,3,2,4,1,0:T(2,128)(2,1)} broadcast(bf16[8,2,2,14,256]{4,2,1,3,0:T(2,128)(2,1)S(1)} %copy.11), dimensions={1,2,3,4,5} | broadcast | bytes 1146880 | tf_op jit(solution)/shard_map/broadcast_in_dim | solution.py:137
  25.8 4.3 %all-to-all-start.1 = ((bf16[4,8,2,2,14,256]{5,3,2,4,1,0:T(2,128)(2,1)}), bf16[4,8,2,2,14,256]{5,3,2,4,1,0:T(2,128)(2,1)S(1)}, u32[]{:S(2)}, u32[]{:S(2)}) async-start(bf16[4,8,2,2,14,256]{5,3,2,4,1,0:T(2,128)(2,1)} %broadcast_in_dim.5), calls=%async_computation.1 | async-start | bytes 1835008 | tf_op jit(solution)/shard_map/all_to_all | solution.py:138
  30.1 0.3 fusion
  30.4 12.9 %all-to-all-done.1 = bf16[4,8,2,2,14,256]{5,3,2,4,1,0:T(2,128)(2,1)S(1)} async-done(((bf16[4,8,2,2,14,256]{5,3,2,4,1,0:T(2,128)(2,1)}), bf16[4,8,2,2,14,256]{5,3,2,4,1,0:T(2,128)(2,1)S(1)}, u32[]{:S(2)}, u32[]{:S(2)}) %all-to-all-start.1) | async-done | bytes 917536 | tf_op jit(solution)/shard_map/all_to_all | solution.py:138
  43.3 0.7 reshape.98
  44.0 1.9 %collective-permute-start.1 = (bf16[448,1024]{1,0:T(8,128)(2,1)S(1)}, bf16[448,1024]{1,0:T(8,128)(2,1)S(1)}, u32[]{:S(2)}, u32[]{:S(2)}) collective-permute-start(bf16[448,1024]{1,0:T(8,128)(2,1)S(1)} %reshape.98), channel_id=1, source_target_pairs={{0,8},{8,0},{1,9},{9,1},{2,10},{10,2},{3,11},{11,3},{4,12},{12,4},... | collective-permute-start | bytes 2752520 | tf_op jit(solution)/shard_map/ppermute | solution.py:177
  45.9 0.5 collective-permute-done
  46.4 1.7 %broadcast_select_fusion.1 = (bf16[8,128,512]{2,1,0:T(8,128)(2,1)S(1)}, bf16[8,128,512]{2,1,0:T(8,128)(2,1)S(1)}) fusion(bf16[8,128,512]{2,1,0:T(8,128)(2,1)} %get-tuple-element.11, bf16[8,128,512]{2,1,0:T(8,128)(2,1)} %collective-permute-done, pred[]{:T(512)S(6)} %eq.21), kind=kLoop, calls=%fused_computation.14 | loop fusion | flops 1048576 | bytes 4194305 | tf_op jit(solution)/shard_map/jit(_where)/select_n | solution.py:180
  48.1 0.3 fusion.2
  48.3 0.1 constant_dynamic-update-slice_fusion.1
  48.4 0.0 collective-permute-done.1
  48.4 0.1 constant_dynamic-update-slice_fusion
  48.5 0.7 convolution_convert_fusion
  49.3 4.5 %collective-permute-start.3 = (bf16[256,896]{1,0:T(8,128)(2,1)S(1)}, bf16[256,896]{1,0:T(8,128)(2,1)S(1)}, u32[]{:S(2)}, u32[]{:S(2)}) collective-permute-start(bf16[256,896]{1,0:T(8,128)(2,1)S(1)} %convolution_convert_fusion), channel_id=1, source_target_pairs={{0,6},{1,3},{2,0},{3,5},{4,2},{5,7},{6,4},{7,1},{8,14},{9,11},{10,... | collective-permute-start | bytes 1376264 | tf_op jit(solution)/shard_map/ppermute | solution.py:188
  53.8 0.7 convolution_convert_fusion.2
  54.5 0.7 convolution_convert_fusion.1
  55.3 1.9 %collective-permute-start.2 = (bf16[256,896]{1,0:T(8,128)(2,1)S(1)}, bf16[256,896]{1,0:T(8,128)(2,1)S(1)}, u32[]{:S(2)}, u32[]{:S(2)}) collective-permute-start(bf16[256,896]{1,0:T(8,128)(2,1)S(1)} %convolution_convert_fusion.2), channel_id=1, source_target_pairs={{0,7},{1,2},{2,1},{3,4},{4,3},{5,6},{6,5},{7,0},{8,15},{9,10},{10,... | collective-permute-start | bytes 1376264 | tf_op jit(solution)/shard_map/ppermute | solution.py:189
  57.2 9.4 %collective-permute-done.3 = bf16[256,896]{1,0:T(8,128)(2,1)S(1)} collective-permute-done((bf16[256,896]{1,0:T(8,128)(2,1)S(1)}, bf16[256,896]{1,0:T(8,128)(2,1)S(1)}, u32[]{:S(2)}, u32[]{:S(2)}) %collective-permute-start.3) | collective-permute-done | bytes 458784 | tf_op jit(solution)/shard_map/ppermute | solution.py:188
  66.6 0.1 add_convert_fusion.1
  66.8 3.3 %collective-permute-start.4 = (bf16[256,896]{1,0:T(8,128)(2,1)S(1)}, bf16[256,896]{1,0:T(8,128)(2,1)S(1)}, u32[]{:S(2)}, u32[]{:S(2)}) collective-permute-start(bf16[256,896]{1,0:T(8,128)(2,1)S(1)} %add_convert_fusion.1), channel_id=1, source_target_pairs={{0,6},{1,3},{2,0},{3,5},{4,2},{5,7},{6,4},{7,1},{8,14},{9,11},{10,... | collective-permute-start | bytes 1376264 | tf_op jit(solution)/shard_map/ppermute | solution.py:190
  70.0 0.7 convolution_convert_fusion.3
  70.8 3.7 %collective-permute-done.2 = bf16[256,896]{1,0:T(8,128)(2,1)S(1)} collective-permute-done((bf16[256,896]{1,0:T(8,128)(2,1)S(1)}, bf16[256,896]{1,0:T(8,128)(2,1)S(1)}, u32[]{:S(2)}, u32[]{:S(2)}) %collective-permute-start.2) | collective-permute-done | bytes 458784 | tf_op jit(solution)/shard_map/ppermute | solution.py:189
  74.5 10.9 %collective-permute-done.4 = bf16[256,896]{1,0:T(8,128)(2,1)S(1)} collective-permute-done((bf16[256,896]{1,0:T(8,128)(2,1)S(1)}, bf16[256,896]{1,0:T(8,128)(2,1)S(1)}, u32[]{:S(2)}, u32[]{:S(2)}) %collective-permute-start.4) | collective-permute-done | bytes 458784 | tf_op jit(solution)/shard_map/ppermute | solution.py:190
  85.4 1.5 %convolution_convert_fusion.4 = bf16[256,896]{1,0:T(8,128)(2,1)} fusion(bf16[896,896]{1,0:T(8,128)(2,1)S(1)} %fusion, bf16[256,896]{1,0:T(8,128)(2,1)S(1)} %collective-permute-done.4, bf16[256,896]{1,0:T(8,128)(2,1)S(1)} %collective-permute-done.2, bf16[256,896]{1,0:T(8,128)(2,1)S(1)} %convolution_convert_fusion.3), kind=kOutput, calls=%fused_computation.12 | convolution fusion | flops 412647424 | bytes 3440640 | tf_op jit(solution)/shard_map/dot_general | solution.py:30
  (1 shorter events, 0.0 us)
Async XLA Ops:
  2.1 22.1 %all-to-all-start = ((bf16[16,2,14,256]{3,1,2,0:T(2,128)(2,1)}), bf16[16,2,14,256]{3,1,2,0:T(2,128)(2,1)S(1)}, u32[]{:S(2)}, u32[]{:S(2)}) async-start(bf16[16,2,14,256]{3,1,2,0:T(2,128)(2,1)} %broadcast_in_dim.4), calls=%async_computation | async-start | bytes 458752 | tf_op jit(solution)/shard_map/all_to_all | solution.py:138
  19.8 26.5 %collective-permute-start = (bf16[8,128,512]{2,1,0:T(8,128)(2,1)}, bf16[8,128,512]{2,1,0:T(8,128)(2,1)}, u32[]{:S(2)}, u32[]{:S(2)}) collective-permute-start(bf16[8,128,512]{2,1,0:T(8,128)(2,1)} %get-tuple-element.12), channel_id=1, source_target_pairs={{0,1},{1,0},{2,3},{3,2},{4,5},{5,4},{6,7},{7,6},{8,9},{9,8},{10,11... | collective-permute-start | bytes 3145736 | tf_op jit(solution)/shard_map/ppermute | solution.py:170
  25.8 17.5 %all-to-all-start.1 = ((bf16[4,8,2,2,14,256]{5,3,2,4,1,0:T(2,128)(2,1)}), bf16[4,8,2,2,14,256]{5,3,2,4,1,0:T(2,128)(2,1)S(1)}, u32[]{:S(2)}, u32[]{:S(2)}) async-start(bf16[4,8,2,2,14,256]{5,3,2,4,1,0:T(2,128)(2,1)} %broadcast_in_dim.5), calls=%async_computation.1 | async-start | bytes 1835008 | tf_op jit(solution)/shard_map/all_to_all | solution.py:138
  44.0 4.5 %collective-permute-start.1 = (bf16[448,1024]{1,0:T(8,128)(2,1)S(1)}, bf16[448,1024]{1,0:T(8,128)(2,1)S(1)}, u32[]{:S(2)}, u32[]{:S(2)}) collective-permute-start(bf16[448,1024]{1,0:T(8,128)(2,1)S(1)} %reshape.98), channel_id=1, source_target_pairs={{0,8},{8,0},{1,9},{9,1},{2,10},{10,2},{3,11},{11,3},{4,12},{12,4},... | collective-permute-start | bytes 2752520 | tf_op jit(solution)/shard_map/ppermute | solution.py:177
  49.3 17.4 %collective-permute-start.3 = (bf16[256,896]{1,0:T(8,128)(2,1)S(1)}, bf16[256,896]{1,0:T(8,128)(2,1)S(1)}, u32[]{:S(2)}, u32[]{:S(2)}) collective-permute-start(bf16[256,896]{1,0:T(8,128)(2,1)S(1)} %convolution_convert_fusion), channel_id=1, source_target_pairs={{0,6},{1,3},{2,0},{3,5},{4,2},{5,7},{6,4},{7,1},{8,14},{9,11},{10,... | collective-permute-start | bytes 1376264 | tf_op jit(solution)/shard_map/ppermute | solution.py:188
  55.3 19.2 %collective-permute-start.2 = (bf16[256,896]{1,0:T(8,128)(2,1)S(1)}, bf16[256,896]{1,0:T(8,128)(2,1)S(1)}, u32[]{:S(2)}, u32[]{:S(2)}) collective-permute-start(bf16[256,896]{1,0:T(8,128)(2,1)S(1)} %convolution_convert_fusion.2), channel_id=1, source_target_pairs={{0,7},{1,2},{2,1},{3,4},{4,3},{5,6},{6,5},{7,0},{8,15},{9,10},{10,... | collective-permute-start | bytes 1376264 | tf_op jit(solution)/shard_map/ppermute | solution.py:189
  66.8 18.6 %collective-permute-start.4 = (bf16[256,896]{1,0:T(8,128)(2,1)S(1)}, bf16[256,896]{1,0:T(8,128)(2,1)S(1)}, u32[]{:S(2)}, u32[]{:S(2)}) collective-permute-start(bf16[256,896]{1,0:T(8,128)(2,1)S(1)} %add_convert_fusion.1), channel_id=1, source_target_pairs={{0,6},{1,3},{2,0},{3,5},{4,2},{5,7},{6,4},{7,1},{8,14},{9,11},{10,... | collective-permute-start | bytes 1376264 | tf_op jit(solution)/shard_map/ppermute | solution.py:190
